TPU v7x, 32 devices: a whole 2x2x4 slice. The times are simulated.
32 devices in a mesh: tensor: 4 (over y, x), context: 8 (over z, core).
Axes of the slice: x: 2, y: 2, z: 4, core: 2. Of those that a mesh axis runs over, the one named last changes fastest.
Arguments:
- query_gate: bfloat16 [1024, 4096], P('context', 'tensor'), may hold values from -6 to 6
- key_gate: bfloat16 [1024, 4096], P('context', 'tensor'), may hold values from -6 to 6
- value_in: bfloat16 [1024, 4096], P('context', 'tensor'), may hold values from -6 to 6
- filter_raw: float32 [1024, 256], P('context', 'tensor'), may hold values from -6 to 6
- grad_out: bfloat16 [1024, 4096], P('context', 'tensor'), may hold values from -6 to 6
Outputs:
- output: bfloat16 [1024, 4096], P('context', 'tensor')
- grad_query: bfloat16 [1024, 4096], P('context', 'tensor')
- grad_key: bfloat16 [1024, 4096], P('context', 'tensor')
- grad_value: bfloat16 [1024, 4096], P('context', 'tensor')
- grad_filter: float32 [1024, 256], P('context', 'tensor')
All inputs are finite; a program needn't handle non-finite values.
Results may differ from a plain program's by a relative error of at most 0.0011.
Values sent between devices are 32-bit elements; how exact they have to be, the bound alone decides.
A program may use at most 64 MiB of HBM per device.

v0:
```python
import math

import jax
import jax.numpy as jnp
from jax import lax
from jax.sharding import PartitionSpec as P

highest = lax.Precision.HIGHEST


def phase_table(count_rows, count_cols, period):
    row_index = lax.broadcasted_iota(jnp.int32, (count_rows, count_cols), 0)
    col_index = lax.broadcasted_iota(jnp.int32, (count_rows, count_cols), 1)
    return (row_index * col_index % period).astype(jnp.float32) * (2.0 * math.pi / period)


def rotate(real_part, imag_part, cosine, sine):
    return (real_part * cosine - imag_part * sine, real_part * sine + imag_part * cosine)


def local(query_gate, key_gate, value_in, filter_raw, grad_out):
    groups = lax.axis_size("context")
    here = lax.axis_index("context")
    rows = query_gate.shape[0]
    width = query_gate.shape[1]
    filter_count = filter_raw.shape[1]
    group_size = width // filter_count
    points = 2 * groups * rows
    scale = 1.0 / math.sqrt(groups * rows)
    local_phase = phase_table(rows, rows, rows)
    cos_local = jnp.cos(local_phase)
    sin_local = jnp.sin(local_phase)
    row_iota = lax.broadcasted_iota(jnp.int32, (1, rows, 1), 1)
    parity = lax.broadcasted_iota(jnp.int32, (2, 1, 1), 0)

    def twiddle_phase(first):
        frequency = 2 * first + parity
        return (row_iota * frequency % points).astype(jnp.float32) * (2.0 * math.pi / points)

    def transpose_forward(signal):
        pieces = lax.all_to_all(signal[None], "context", split_axis=1, concat_axis=0, tiled=True)
        angles = phase_table(2 * groups, groups, 2 * groups)
        spread_re = jnp.einsum("ap,plc->alc", jnp.cos(angles), pieces, precision=highest)
        spread_im = -jnp.einsum("ap,plc->alc", jnp.sin(angles), pieces, precision=highest)
        return lax.all_to_all(
            jnp.stack([spread_re, spread_im]), "context", split_axis=1, concat_axis=2, tiled=True
        )

    def forward(signal):
        spec = transpose_forward(signal)
        phase = twiddle_phase(here)
        tw_re, tw_im = rotate(spec[0], spec[1], jnp.cos(phase), -jnp.sin(phase))
        out_re = jnp.einsum("br,erc->ebc", cos_local, tw_re, precision=highest) + jnp.einsum(
            "br,erc->ebc", sin_local, tw_im, precision=highest
        )
        out_im = jnp.einsum("br,erc->ebc", cos_local, tw_im, precision=highest) - jnp.einsum(
            "br,erc->ebc", sin_local, tw_re, precision=highest
        )
        return jnp.stack([out_re, out_im])

    def transpose_inverse(spec):
        pieces = lax.all_to_all(spec, "context", split_axis=2, concat_axis=1, tiled=True)
        angles = phase_table(groups, 2 * groups, 2 * groups)
        values = jnp.einsum(
            "pa,alc->plc", jnp.cos(angles), pieces[0], precision=highest
        ) - jnp.einsum("pa,alc->plc", jnp.sin(angles), pieces[1], precision=highest)
        return lax.all_to_all(values, "context", split_axis=0, concat_axis=1, tiled=True)[0]

    def turned(spec, first):
        loc_re = jnp.einsum("rb,ebc->erc", cos_local, spec[0], precision=highest) - jnp.einsum(
            "rb,ebc->erc", sin_local, spec[1], precision=highest
        )
        loc_im = jnp.einsum("rb,ebc->erc", cos_local, spec[1], precision=highest) + jnp.einsum(
            "rb,ebc->erc", sin_local, spec[0], precision=highest
        )
        phase = twiddle_phase(first)
        rot_re, rot_im = rotate(loc_re, loc_im, jnp.cos(phase), jnp.sin(phase))
        return jnp.stack([rot_re, rot_im])

    def inverse(spec):
        signal = transpose_inverse(turned(spec, here))
        return signal * (1.0 / points)

    def widen(part):
        spread = jnp.broadcast_to(part[..., None], part.shape + (group_size,))
        return spread.reshape(part.shape[:-1] + (width,))

    def group_total(part):
        return jnp.sum(part.reshape(part.shape[:-1] + (filter_count, group_size)), axis=-1)

    query_full = query_gate.astype(jnp.float32)
    key_full = key_gate.astype(jnp.float32)
    value_full = value_in.astype(jnp.float32)
    grad_full = grad_out.astype(jnp.float32)
    gated = key_full * value_full
    grad_conv = grad_full * query_full
    filt_part = filter_raw * scale
    spec_gated = forward(gated)
    spec_grad = forward(grad_conv)
    spec_filt = forward(filt_part)
    gated_re, gated_im = (spec_gated[0], spec_gated[1])
    filt_re, filt_im = (widen(spec_filt[0]), widen(spec_filt[1]))
    grad_re, grad_im = (spec_grad[0], spec_grad[1])
    conv_spec = jnp.stack(
        [gated_re * filt_re - gated_im * filt_im, gated_re * filt_im + gated_im * filt_re]
    )
    back_spec = jnp.stack(
        [filt_re * grad_re + filt_im * grad_im, filt_re * grad_im - filt_im * grad_re]
    )
    corr_spec = jnp.stack(
        [
            group_total(gated_re * grad_re + gated_im * grad_im),
            group_total(gated_re * grad_im - gated_im * grad_re),
        ]
    )
    conv = inverse(conv_spec)
    grad_gated = inverse(back_spec)
    corr = inverse(corr_spec)
    output = (query_full * conv).astype(jnp.bfloat16)
    grad_query = (grad_full * conv).astype(jnp.bfloat16)
    grad_key = (grad_gated * value_full).astype(jnp.bfloat16)
    grad_value = (grad_gated * key_full).astype(jnp.bfloat16)
    grad_filter = corr * scale
    return (output, grad_query, grad_key, grad_value, grad_filter)


def solution(mesh):
    return jax.shard_map(
        local,
        mesh=mesh,
        in_specs=(
            P("context", "tensor"),
            P("context", "tensor"),
            P("context", "tensor"),
            P("context", "tensor"),
            P("context", "tensor"),
        ),
        out_specs=(
            P("context", "tensor"),
            P("context", "tensor"),
            P("context", "tensor"),
            P("context", "tensor"),
            P("context", "tensor"),
        ),
        check_vma=False,
    )
```

profile of v0, /device:TPU:0, one launch (start us, length us, event | category | flops | bytes accessed | tf_op | source)
XLA Modules:
  0.0 381.7 jit_solution(14372812453379356640)
XLA Ops:
  0.6 0.8 copy.107
  2.0 0.8 reduce
  3.5 6.3 %all-to-all-start.2 = ((f32[8,1,1024]{2,1,0:T(1,128)}), f32[8,1,1024]{2,1,0:T(1,128)S(1)}, u32[]{:S(2)}, u32[]{:S(2)}) async-start(f32[8,1,1024]{2,1,0:T(1,128)} %reshape.177), calls=%async_computation.2 | async-start | bytes 65536 | tf_op jit(solution)/shard_map/all_to_all | solution.py:41
  9.9 1.1 fusion.18
  11.0 1.3 copy.123
  12.3 3.3 all-to-all-done.2
  15.6 3.5 all-to-all-start.6
  19.1 0.7 reduce.1
  20.8 0.8 reshape.179
  21.7 12.7 %all-to-all-done.6 = f32[1,128,1024]{2,0,1:T(1,128)S(1)} async-done(((f32[1,128,1024]{2,0,1:T(1,128)}), f32[1,128,1024]{2,0,1:T(1,128)S(1)}, u32[]{:S(2)}, u32[]{:S(2)}) %all-to-all-start.6) | async-done | bytes 524320 | tf_op jit(solution)/shard_map/all_to_all | solution.py:41
  34.4 3.4 all-to-all-start.3
  37.9 1.2 fusion
  39.1 1.2 convolution_bitcast_fusion
  40.5 2.6 copy.126
  43.1 1.4 all-to-all-done.3
  44.5 3.8 all-to-all-start.7
  48.4 1.0 reduce.2
  51.9 45.3 %all-to-all-done.7 = f32[2,16,16,1024]{3,2,0,1:T(8,128)S(1)} async-done(((f32[2,16,16,1024]{3,2,0,1:T(8,128)}), f32[2,16,16,1024]{3,2,0,1:T(8,128)S(1)}, u32[]{:S(2)}, u32[]{:S(2)}) %all-to-all-start.7) | async-done | bytes 2097184 | tf_op jit(solution)/shard_map/all_to_all | solution.py:45
  97.8 2.0 fusion.26
  99.9 2.0 fusion.25
  101.9 2.1 fusion.2
  104.0 3.1 fusion.11
  107.1 1.2 fusion.48
  108.3 1.6 fusion.46
  110.0 1.2 convolution_add_fusion
  111.2 1.4 subtract_bitcast_fusion
  112.8 2.5 copy.134
  115.2 52.6 %all_to_all.153 = f32[2,2,128,1024]{3,1,0,2:T(2,128)S(1)} all-to-all(f32[2,2,128,1024]{3,1,0,2:T(2,128)} %copy.134), channel_id=1, replica_groups=mesh['tensor'=4,'context'=8] {'context'}, dimensions={2} | all-to-all | bytes 4194304 | tf_op jit(solution)/shard_map/all_to_all | solution.py:62
  167.8 1.2 copy.135
  169.0 1.2 fusion.286
  170.2 0.8 copy.137
  171.8 2.0 copy.136
  173.8 1.7 squeeze.47
  175.5 1.9 fusion.110
  178.3 17.8 %all_to_all.154 = f32[8,16,1024]{2,1,0:T(8,128)S(1)} all-to-all(f32[8,16,1024]{2,1,0:T(8,128)S(1)} %copy.138), channel_id=1, replica_groups=mesh['tensor'=4,'context'=8] {'context'}, dimensions={0} | all-to-all | bytes 1048576 | tf_op jit(solution)/shard_map/all_to_all | solution.py:67
  196.2 0.9 fusion.14
  197.7 17.9 %all_to_all.155 = f32[1,128,1024]{2,0,1:T(1,128)S(1)} all-to-all(f32[1,128,1024]{2,0,1:T(1,128)S(1)} %copy.98), channel_id=1, replica_groups=mesh['tensor'=4,'context'=8] {'context'}, dimensions={1} | all-to-all | bytes 1048576 | tf_op jit(solution)/shard_map/all_to_all | solution.py:41
  215.7 1.2 fusion.1
  216.9 1.2 convolution_bitcast_fusion.1
  218.4 1.2 copy.101
  219.6 51.5 %all_to_all.156 = f32[2,16,16,1024]{3,2,0,1:T(8,128)S(1)} all-to-all(f32[2,16,16,1024]{3,2,0,1:T(8,128)S(1)} %copy.101), channel_id=1, replica_groups=mesh['tensor'=4,'context'=8] {'context'}, dimensions={1} | all-to-all | bytes 4194304 | tf_op jit(solution)/shard_map/all_to_all | solution.py:45
  271.7 2.0 fusion.24
  273.8 2.0 fusion.23
  275.8 2.0 fusion.4
  277.9 2.1 fusion.9
  280.0 0.7 bitcast_reduce_fusion.1
  283.0 0.9 reshape.181
  283.9 3.6 all-to-all-start.10
  287.5 1.2 fusion.54
  288.8 1.2 fusion.52
  290.0 1.2 convolution_add_fusion.2
  291.3 1.4 subtract_bitcast_fusion.1
  292.8 2.5 copy.118
  295.3 5.1 %all-to-all-start.4 = ((f32[2,2,128,1024]{3,1,0,2:T(2,128)}), f32[2,2,128,1024]{3,1,0,2:T(2,128)S(1)}, u32[]{:S(2)}, u32[]{:S(2)}) async-start(f32[2,2,128,1024]{3,1,0,2:T(2,128)} %copy.118), calls=%async_computation.4 | async-start | bytes 4194304 | tf_op jit(solution)/shard_map/all_to_all | solution.py:62
  300.3 1.0 reduce.3
  303.0 46.4 %all-to-all-done.4 = f32[2,2,128,1024]{3,1,0,2:T(2,128)S(1)} async-done(((f32[2,2,128,1024]{3,1,0,2:T(2,128)}), f32[2,2,128,1024]{3,1,0,2:T(2,128)S(1)}, u32[]{:S(2)}, u32[]{:S(2)}) %all-to-all-start.4) | async-done | bytes 2097184 | tf_op jit(solution)/shard_map/all_to_all | solution.py:62
  349.4 3.6 all-to-all-start.11
  353.0 1.2 copy.119
  354.5 0.8 copy.121
  356.0 0.8 copy.120
  358.9 1.1 copy.122
  360.0 5.1 %all-to-all-start.5 = ((f32[8,16,1024]{2,1,0:T(8,128)}), f32[8,16,1024]{2,1,0:T(8,128)S(1)}, u32[]{:S(2)}, u32[]{:S(2)}) async-start(f32[8,16,1024]{2,1,0:T(8,128)} %copy.122), calls=%async_computation.5 | async-start | bytes 1048576 | tf_op jit(solution)/shard_map/all_to_all | solution.py:67
  366.6 13.8 %all-to-all-done.5 = f32[8,16,1024]{2,1,0:T(8,128)S(1)} async-done(((f32[8,16,1024]{2,1,0:T(8,128)}), f32[8,16,1024]{2,1,0:T(8,128)S(1)}, u32[]{:S(2)}, u32[]{:S(2)}) %all-to-all-start.5) | async-done | bytes 524320 | tf_op jit(solution)/shard_map/all_to_all | solution.py:67
  380.5 0.9 fusion.17
  (73 shorter events, 17.6 us)
Async XLA Ops:
  3.5 12.1 %all-to-all-start.2 = ((f32[8,1,1024]{2,1,0:T(1,128)}), f32[8,1,1024]{2,1,0:T(1,128)S(1)}, u32[]{:S(2)}, u32[]{:S(2)}) async-start(f32[8,1,1024]{2,1,0:T(1,128)} %reshape.177), calls=%async_computation.2 | async-start | bytes 65536 | tf_op jit(solution)/shard_map/all_to_all | solution.py:41
  15.6 18.8 %all-to-all-start.6 = ((f32[1,128,1024]{2,0,1:T(1,128)}), f32[1,128,1024]{2,0,1:T(1,128)S(1)}, u32[]{:S(2)}, u32[]{:S(2)}) async-start(f32[1,128,1024]{2,0,1:T(1,128)} %copy.123), calls=%async_computation.6 | async-start | bytes 1048576 | tf_op jit(solution)/shard_map/all_to_all | solution.py:41
  34.4 10.1 %all-to-all-start.3 = ((f32[8,1,4096]{2,1,0:T(1,128)}), f32[8,1,4096]{2,1,0:T(1,128)S(1)}, u32[]{:S(2)}, u32[]{:S(2)}) async-start(f32[8,1,4096]{2,1,0:T(1,128)} %reshape.179), calls=%async_computation.3 | async-start | bytes 262144 | tf_op jit(solution)/shard_map/all_to_all | solution.py:45
  44.5 52.7 %all-to-all-start.7 = ((f32[2,16,16,1024]{3,2,0,1:T(8,128)}), f32[2,16,16,1024]{3,2,0,1:T(8,128)S(1)}, u32[]{:S(2)}, u32[]{:S(2)}) async-start(f32[2,16,16,1024]{3,2,0,1:T(8,128)} %copy.126), calls=%async_computation.7 | async-start | bytes 4194304 | tf_op jit(solution)/shard_map/all_to_all | solution.py:45
  178.0 18.2 %copy-start.3 = (bf16[128,1024]{1,0:T(8,128)(2,1)S(1)}, bf16[128,1024]{1,0:T(8,128)(2,1)}, u32[]{:S(2)}) copy-start(bf16[128,1024]{1,0:T(8,128)(2,1)} %param.6) | copy-start | bytes 786436
  178.0 18.2 %copy-start.4 = (bf16[128,1024]{1,0:T(8,128)(2,1)S(1)}, bf16[128,1024]{1,0:T(8,128)(2,1)}, u32[]{:S(2)}) copy-start(bf16[128,1024]{1,0:T(8,128)(2,1)} %param.7) | copy-start | bytes 786436
  277.9 2.2 copy-start
  283.9 11.3 %all-to-all-start.10 = ((f32[8,1,4096]{2,1,0:T(1,128)}), f32[8,1,4096]{2,1,0:T(1,128)S(1)}, u32[]{:S(2)}, u32[]{:S(2)}) async-start(f32[8,1,4096]{2,1,0:T(1,128)} %reshape.181), calls=%async_computation.10 | async-start | bytes 262144 | tf_op jit(solution)/shard_map/all_to_all | solution.py:62
  295.3 54.1 %all-to-all-start.4 = ((f32[2,2,128,1024]{3,1,0,2:T(2,128)}), f32[2,2,128,1024]{3,1,0,2:T(2,128)S(1)}, u32[]{:S(2)}, u32[]{:S(2)}) async-start(f32[2,2,128,1024]{3,1,0,2:T(2,128)} %copy.118), calls=%async_computation.4 | async-start | bytes 4194304 | tf_op jit(solution)/shard_map/all_to_all | solution.py:62
  349.4 10.6 %all-to-all-start.11 = ((f32[8,1,1024]{2,1,0:T(1,128)}), f32[8,1,1024]{2,1,0:T(1,128)S(1)}, u32[]{:S(2)}, u32[]{:S(2)}) async-start(f32[8,1,1024]{2,1,0:T(1,128)} %reshape.183), calls=%async_computation.11 | async-start | bytes 65536 | tf_op jit(solution)/shard_map/all_to_all | solution.py:67
  358.9 21.6 %copy-start.1 = (bf16[128,1024]{1,0:T(8,128)(2,1)S(1)}, bf16[128,1024]{1,0:T(8,128)(2,1)}, u32[]{:S(2)}) copy-start(bf16[128,1024]{1,0:T(8,128)(2,1)} %param.9) | copy-start | bytes 786436
  358.9 21.6 %copy-start.2 = (bf16[128,1024]{1,0:T(8,128)(2,1)S(1)}, bf16[128,1024]{1,0:T(8,128)(2,1)}, u32[]{:S(2)}) copy-start(bf16[128,1024]{1,0:T(8,128)(2,1)} %param.5) | copy-start | bytes 786436
  360.0 20.4 %all-to-all-start.5 = ((f32[8,16,1024]{2,1,0:T(8,128)}), f32[8,16,1024]{2,1,0:T(8,128)S(1)}, u32[]{:S(2)}, u32[]{:S(2)}) async-start(f32[8,16,1024]{2,1,0:T(8,128)} %copy.122), calls=%async_computation.5 | async-start | bytes 1048576 | tf_op jit(solution)/shard_map/all_to_all | solution.py:67
where the time goes:
time: 388 us; the launch traced here: 382 us
  blocking collectives  140 us (36%)
  waiting for transfers between devices  123 us (32%)
  matrix products  42.4 us (11%)
  starting transfers between devices  34.3 us (9%)
  local copies, waits for them, and re-layouts  31.8 us (8%)
  other arithmetic  8.83 us (2%)
    all_to_all x1, blocking collectives, transpose_inverse(): lax.all_to_all(spec, 'context', split_axis=2, concat_axis=1, tiled=True)  52.6 us
    all_to_all x1, blocking collectives, transpose_forward(): lax.all_to_all(jnp.stack([spread_re, spread_im]), 'context', split_axis=1...  51.5 us
    all_to_all x2, waiting for transfers between devices, transpose_forward(): lax.all_to_all(jnp.stack([spread_re, spread_im]), 'context', split_axis=1...  46.7 us
    all_to_all x2, waiting for transfers between devices, transpose_inverse(): lax.all_to_all(spec, 'context', split_axis=2, concat_axis=1, tiled=True)  46.4 us
    all_to_all x1, blocking collectives, transpose_forward(): lax.all_to_all(signal[None], 'context', split_axis=1, concat_axis=0, tile...  17.9 us
    all_to_all x1, blocking collectives, transpose_inverse(): lax.all_to_all(values, 'context', split_axis=0, concat_axis=1, tiled=True)  17.8 us
    all_to_all x2, waiting for transfers between devices, transpose_forward(): lax.all_to_all(signal[None], 'context', split_axis=1, concat_axis=0, tile...  16 us
    all_to_all x2, waiting for transfers between devices, transpose_inverse(): lax.all_to_all(values, 'context', split_axis=0, concat_axis=1, tiled=True)  13.8 us
  transfers between devices with their start and end apart: 8, of which 6 were waited for; matrix products, arithmetic and copies ran while one was open for 9% of the time, Pallas kernels for 0%

commit v1 on v0

--- a/solution.py
+++ b/solution.py
@@ -1,8 +1,12 @@
+import functools
 import math
 
 import jax
 import jax.numpy as jnp
+import numpy as np
 from jax import lax
+from jax.experimental import pallas as pl
+from jax.experimental.pallas import tpu as pltpu
 from jax.sharding import PartitionSpec as P
 
 highest = lax.Precision.HIGHEST
@@ -124,9 +128,363 @@
     return (output, grad_query, grad_key, grad_value, grad_filter)
 
 
+LANES = 128
+VMEM_BUDGET = 40 * 2**20
+
+
+def halves(table):
+    high = jnp.asarray(table, jnp.float32).astype(jnp.bfloat16)
+    low = (jnp.asarray(table, jnp.float32) - high.astype(jnp.float32)).astype(jnp.bfloat16)
+    return high, low
+
+
+def np_halves(table):
+    table = table.astype(np.float32)
+    high = table.astype(jnp.bfloat16)
+    low = (table - high.astype(np.float32)).astype(jnp.bfloat16)
+    return high, low
+
+
+def tables(block):
+    k = np.arange(block, dtype=np.float64)[:, None] + 0.5
+    n = np.arange(-block, block, dtype=np.float64)[None, :]
+    angle = (np.pi / block) * k * n
+    return np.concatenate([np.cos(angle), -np.sin(angle)], axis=0)
+
+
+NN = (((1,), (0,)), ((), ()))
+NT = (((1,), (1,)), ((), ()))
+
+
+def dot(a, b, dims=NN):
+    return lax.dot_general(a, b, dims, preferred_element_type=jnp.float32)
+
+
+def dot3(a, b, dims=NN):
+    return dot(a[0], b[0], dims) + dot(a[0], b[1], dims) + dot(a[1], b[0], dims)
+
+
+def kernel(chips, q_ref, k_ref, v_ref, go_ref, filt_ref, fwd_hi, fwd_lo, inv_hi, inv_lo, spread_ref,
+           conv_ref, gg_ref, gf_ref,
+           g_buf, r_buf, sg_buf, h_buf, h_spec, conv_acc, gg_acc, r_spec, c_spec, y_buf, x_buf, c_own, c_buf, f_buf,
+           f_send, f_recv, e_send, e_recv, g_send, g_recv, r_send, r_recv, y_send, y_recv, c_send, c_recv, p_send, p_recv):
+    groups = 2 * chips
+    rows = q_ref.shape[0]
+    half = q_ref.shape[1] // 2
+    block = 2 * rows
+    chunks = half // LANES
+    nf = filt_ref.shape[0] // 2
+    me = lax.axis_index("context")
+    z, c = me // 2, me % 2
+    partner = z * 2 + (1 - c)
+    right = (me + 2) % groups
+    left = (me + groups - 2) % groups
+
+    def remote(src, dst, send, recv, target):
+        return pltpu.make_async_remote_copy(
+            src_ref=src, dst_ref=dst, send_sem=send, recv_sem=recv,
+            device_id={"context": target}, device_id_type=pl.DeviceIdType.MESH)
+
+    def columns(which, j):
+        return pl.ds(pl.multiple_of(which * half + j * LANES, LANES), LANES)
+
+    my_rows = pl.ds(pl.multiple_of(c * rows, rows), rows)
+    its_rows = pl.ds(pl.multiple_of((1 - c) * rows, rows), rows)
+
+    barrier = pltpu.get_barrier_semaphore()
+    for d in range(1, groups):
+        pl.semaphore_signal(barrier, inc=1, device_id={"context": (me + d) % groups},
+                            device_id_type=pl.DeviceIdType.MESH)
+    pl.semaphore_wait(barrier, groups - 1)
+
+    def swap(which, j):
+        buf = g_buf if which == 0 else r_buf
+        return remote(sg_buf.at[which, j], buf.at[0, j, my_rows, :],
+                      e_send.at[which, j], e_recv.at[which, j], partner)
+
+    def gate_out(j, carry):
+        cols = columns(1 - c, j)
+        sg_buf[0, j] = k_ref[:, cols].astype(jnp.float32) * v_ref[:, cols].astype(jnp.float32)
+        swap(0, j).start()
+        sg_buf[1, j] = go_ref[:, cols].astype(jnp.float32) * q_ref[:, cols].astype(jnp.float32)
+        swap(1, j).start()
+        return carry
+
+    lax.fori_loop(0, chunks, gate_out, 0)
+
+    def filter_copy(d):
+        target = (me + d) % groups
+        part = pl.ds(pl.multiple_of((target % 2) * nf, nf), nf)
+        return remote(filt_ref.at[part, :], h_buf.at[z, c], f_send.at[d], f_recv.at[d], target)
+
+    for d in range(1, groups):
+        filter_copy(d).start()
+    h_buf[z, c] = filt_ref[pl.ds(pl.multiple_of(c * nf, nf), nf), :]
+
+    def gate_own(j, carry):
+        cols = columns(c, j)
+        g_buf[0, j, my_rows, :] = k_ref[:, cols].astype(jnp.float32) * v_ref[:, cols].astype(jnp.float32)
+        r_buf[0, j, my_rows, :] = go_ref[:, cols].astype(jnp.float32) * q_ref[:, cols].astype(jnp.float32)
+        return carry
+
+    lax.fori_loop(0, chunks, gate_own, 0)
+
+    def g_copy(s, j):
+        return remote(g_buf.at[s, j], g_buf.at[s + 1, j], g_send.at[s, j], g_recv.at[s, j], right)
+
+    def r_copy(s, j):
+        return remote(r_buf.at[s, j], r_buf.at[s + 1, j], r_send.at[s, j], r_recv.at[s, j], left)
+
+    def first_sends(j, carry):
+        swap(0, j).wait_recv()
+
+        @pl.when(z + 1 < chips)
+        def _():
+            g_copy(0, j).start()
+
+        swap(1, j).wait_recv()
+
+        @pl.when(z >= 1)
+        def _():
+            r_copy(0, j).start()
+        return carry
+
+    lax.fori_loop(0, chunks, first_sends, 0)
+
+    for d in range(1, groups):
+        filter_copy(d).wait_recv()
+
+    def lag_spectrum(m, carry):
+        late = jnp.concatenate([h_buf[m, 0], h_buf[m, 1]], axis=1)
+        before = jnp.maximum(m - 1, 0)
+        early = jnp.concatenate([h_buf[before, 0], h_buf[before, 1]], axis=1)
+        early = early * (m > 0).astype(jnp.float32)
+        window = halves(jnp.concatenate([early, late], axis=1))
+        spec = halves(dot3((fwd_hi[...], fwd_lo[...]), window, NT))
+
+        def widen(j, inner):
+            h_spec[m, j] = dot(spec[0], spread_ref[j]) + dot(spec[1], spread_ref[j])
+            return inner
+
+        lax.fori_loop(0, chunks, widen, 0)
+        return carry
+
+    lax.fori_loop(0, chips, lag_spectrum, 0)
+    c_spec[...] = jnp.zeros_like(c_spec)
+
+    def spectrum(signal):
+        return dot3((fwd_hi[:, block:], fwd_lo[:, block:]), halves(signal))
+
+    def conj_times(a, b):
+        ar, ai, br, bi = a[:block], a[block:], b[:block], b[block:]
+        return jnp.concatenate([ar * br + ai * bi, ar * bi - ai * br], axis=0)
+
+    def times(a, b):
+        ar, ai, br, bi = a[:block], a[block:], b[:block], b[block:]
+        return jnp.concatenate([ar * br - ai * bi, ar * bi + ai * br], axis=0)
+
+    def add_corr(m, j, g):
+        prod = halves(conj_times(g, r_spec[j]))
+        c_spec[m] += dot(spread_ref[j], prod[0], NT) + dot(spread_ref[j], prod[1], NT)
+
+    def own_step(j, carry):
+        r = spectrum(r_buf[0, j])
+        r_spec[j] = r
+        gg_acc[j] = conj_times(h_spec[0, j], r)
+        g = spectrum(g_buf[0, j])
+        conv_acc[j] = times(h_spec[0, j], g)
+        add_corr(0, j, g)
+        return carry
+
+    lax.fori_loop(0, chunks, own_step, 0)
+
+    def y_copy(which, j):
+        return remote(y_buf.at[which, j, its_rows, :], x_buf.at[which, j],
+                      y_send.at[which, j], y_recv.at[which, j], partner)
+
+    def finish(j):
+        for which, acc, out in ((0, conv_acc, conv_ref), (1, gg_acc, gg_ref)):
+            y_buf[which, j] = dot3((inv_hi[...], inv_lo[...]), halves(acc[j]))
+            y_copy(which, j).start()
+            out[:, columns(c, j)] = y_buf[which, j, my_rows, :]
+
+    for s in range(chips - 1):
+        def step(j, carry):
+            @pl.when(z - 1 - s >= 0)
+            def _():
+                g_copy(s, j).wait_recv()
+                if s < chips - 2:
+                    @pl.when(z + 1 < chips)
+                    def _():
+                        g_copy(s + 1, j).start()
+                g = spectrum(g_buf[s + 1, j])
+                conv_acc[j] += times(h_spec[s + 1, j], g)
+                add_corr(s + 1, j, g)
+
+            @pl.when(z + 1 + s < chips)
+            def _():
+                r_copy(s, j).wait_recv()
+                if s < chips - 2:
+                    @pl.when(z >= 1)
+                    def _():
+                        r_copy(s + 1, j).start()
+                gg_acc[j] += conj_times(h_spec[s + 1, j], spectrum(r_buf[s + 1, j]))
+
+            if s == chips - 2:
+                finish(j)
+            return carry
+
+        lax.fori_loop(0, chunks, step, 0)
+
+    def lag_block(n):
+        here = dot3(halves(c_spec[n]), (fwd_hi[:, block:], fwd_lo[:, block:]))
+        after = dot3(halves(c_spec[n + 1]), (fwd_hi[:, :block], fwd_lo[:, :block]))
+        return (here + after) * (1.0 / block)
+
+    def c_copy(n):
+        return remote(c_own.at[n], c_buf.at[z], c_send.at[n], c_recv.at[z], n * 2 + c)
+
+    for n in range(chips):
+        @pl.when(n <= z)
+        def _():
+            total = lag_block(n)
+            c_own[n, 0] = total[:, :rows]
+            c_own[n, 1] = total[:, rows:]
+
+        @pl.when(n < z)
+        def _():
+            c_copy(n).start()
+
+    for i in range(1, chips):
+        @pl.when(i > z)
+        def _():
+            remote(c_own.at[0], c_buf.at[i], c_send.at[0], c_recv.at[i], partner).wait_recv()
+            c_own[z] += c_buf[i]
+
+    last = remote(c_own.at[z, 1 - c], f_buf, p_send, p_recv, partner)
+    last.start()
+    gf_ref[pl.ds(pl.multiple_of(c * nf, nf), nf), :] = c_own[z, c]
+
+    def place(j, carry):
+        for which, out in ((0, conv_ref), (1, gg_ref)):
+            y_copy(which, j).wait_recv()
+            out[:, columns(1 - c, j)] = x_buf[which, j]
+        return carry
+
+    lax.fori_loop(0, chunks, place, 0)
+    last.wait_recv()
+    gf_ref[pl.ds(pl.multiple_of((1 - c) * nf, nf), nf), :] = f_buf[...]
+
+    last.wait_send()
+    for n in range(chips - 1):
+        @pl.when(n < z)
+        def _():
+            c_copy(n).wait_send()
+    for d in range(1, groups):
+        filter_copy(d).wait_send()
+
+    def drain(j, carry):
+        for which in range(2):
+            swap(which, j).wait_send()
+            y_copy(which, j).wait_send()
+        for s in range(chips - 1):
+            @pl.when((z - s >= 0) & (z + 1 < chips))
+            def _():
+                g_copy(s, j).wait_send()
+
+            @pl.when((z + s < chips) & (z >= 1))
+            def _():
+                r_copy(s, j).wait_send()
+        return carry
+
+    lax.fori_loop(0, chunks, drain, 0)
+
+
+def scratch(chips, rows, half, nf):
+    chunks, block = half // LANES, 2 * rows
+    f32 = jnp.float32
+    memory = [
+        (chips, chunks, block, LANES),
+        (chips, chunks, block, LANES),
+        (2, chunks, rows, LANES),
+        (chips, 2, nf, rows),
+        (chips, chunks, 2 * block, LANES),
+        (chunks, 2 * block, LANES),
+        (chunks, 2 * block, LANES),
+        (chunks, 2 * block, LANES),
+        (chips + 1, nf, 2 * block),
+        (2, chunks, block, LANES),
+        (2, chunks, rows, LANES),
+        (chips, 2, nf, rows),
+        (chips, 2, nf, rows),
+        (nf, rows),
+    ]
+    steps = max(chips - 1, 1)
+    sems = [
+        (2 * chips,), (2 * chips,), (2, chunks), (2, chunks), (steps, chunks), (steps, chunks),
+        (steps, chunks), (steps, chunks), (2, chunks), (2, chunks), (chips,), (chips,),
+    ]
+    used = sum(4 * math.prod(shape) for shape in memory)
+    specs = [pltpu.VMEM(shape, f32) for shape in memory]
+    specs += [pltpu.SemaphoreType.DMA(shape) for shape in sems]
+    specs += [pltpu.SemaphoreType.DMA, pltpu.SemaphoreType.DMA]
+    return used, specs
+
+
+def fits(chips, rows, width, filters):
+    used, _ = scratch(chips, rows, width // 2, filters // 2)
+    aligned = rows % LANES == 0 and width % (2 * LANES) == 0 and filters % 16 == 0
+    return aligned and chips >= 2 and used <= VMEM_BUDGET // 2
+
+
+def local_fast(query_gate, key_gate, value_in, filter_raw, grad_out):
+    groups = lax.axis_size("context")
+    chips = groups // 2
+    rows, width = query_gate.shape
+    filters = filter_raw.shape[1]
+    half, nf, block = width // 2, filters // 2, 2 * rows
+    chunks = half // LANES
+    scale = 1.0 / math.sqrt(groups * rows)
+    forward = tables(block)
+    fwd = np_halves(forward)
+    inv = np_halves(forward[:, block:].T / block)
+    spread = np.kron(np.eye(nf), np.ones((1, width // filters)))
+    spread = spread.reshape(nf, chunks, LANES).transpose(1, 0, 2).astype(jnp.bfloat16)
+    _, scratches = scratch(chips, rows, half, nf)
+    vmem = pl.BlockSpec(memory_space=pltpu.VMEM)
+    conv, grad_gated, corr = pl.pallas_call(
+        functools.partial(kernel, chips),
+        out_shape=(
+            jax.ShapeDtypeStruct((rows, width), jnp.float32),
+            jax.ShapeDtypeStruct((rows, width), jnp.float32),
+            jax.ShapeDtypeStruct((filters, rows), jnp.float32),
+        ),
+        in_specs=[vmem] * 10,
+        out_specs=(vmem,) * 3,
+        scratch_shapes=scratches,
+        compiler_params=pltpu.CompilerParams(
+            collective_id=0, has_side_effects=True, vmem_limit_bytes=VMEM_BUDGET),
+        cost_estimate=pl.CostEstimate(flops=10**10, bytes_accessed=8 * 2**20, transcendentals=0),
+        name="ring_conv",
+    )(query_gate, key_gate, value_in, grad_out, (filter_raw * scale).T, *fwd, *inv, spread)
+    output = (query_gate.astype(jnp.float32) * conv).astype(jnp.bfloat16)
+    grad_query = (grad_out.astype(jnp.float32) * conv).astype(jnp.bfloat16)
+    grad_key = (grad_gated * value_in.astype(jnp.float32)).astype(jnp.bfloat16)
+    grad_value = (grad_gated * key_gate.astype(jnp.float32)).astype(jnp.bfloat16)
+    return output, grad_query, grad_key, grad_value, corr.T * scale
+
+
+def dispatch(query_gate, key_gate, value_in, filter_raw, grad_out):
+    args = (query_gate, key_gate, value_in, filter_raw, grad_out)
+    rows, width = query_gate.shape
+    if fits(lax.axis_size("context") // 2, rows, width, filter_raw.shape[1]):
+        return local_fast(*args)
+    return local(*args)
+
+
 def solution(mesh):
     return jax.shard_map(
-        local,
+        dispatch,
         mesh=mesh,
         in_specs=(
             P("context", "tensor"),

time: 388 us -> 61.5 us (0.16); the launches traced: 382 us -> 61 us
  blocking collectives: 140 us -> 0 us
  waiting for transfers between devices: 123 us -> 0 us
  Pallas kernels: 0 us -> 50 us
  matrix products: 42.4 us -> 0 us
  starting transfers between devices: 34.3 us -> 0 us
  local copies, waits for them, and re-layouts: 31.8 us -> 7.79 us
  other arithmetic: 8.83 us -> 2.54 us
    all_to_all x4 -> x0, blocking collectives: 140 us -> none  [the longest x1 52.6 us: transpose_inverse(): lax.all_to_all(spec, 'context', split_axis=2, concat_axis=1, tiled=True)]
    all_to_all x8 -> x0, waiting for transfers between devices: 123 us -> none  [the longest x2 46.7 us: transpose_forward(): lax.all_to_all(jnp.stack([spread_re, spread_im]), 'context', split_axis=1...]
    pallas_call x0 -> x1, Pallas kernels: none -> 50 us  [local_fast(): pl.pallas_call(functools.partial(kernel, chips), out_shape=(jax.ShapeDtyp...]
    dot_general x36 -> x0, matrix products: 42.4 us -> none  [the longest x3 5.85 us: forward(): jnp.einsum('br,erc->ebc', sin_local, tw_im, precision=highest)]
    all_to_all x8 -> x0, starting transfers between devices: 34.3 us -> none  [the longest x2 9.82 us: transpose_forward(): lax.all_to_all(signal[None], 'context', split_axis=1, concat_axis=0, tile...]
    another operation x6 -> x0, local copies, waits for them, and re-layouts: 8.97 us -> none  [the longest x3 5.11 us: turned(): return jnp.stack([rot_re, rot_im])]
    slice x16 -> x0, local copies, waits for them, and re-layouts: 6.82 us -> none  [the longest x6 3.16 us: transpose_inverse(): pieces[1]]
    unnamed x23 -> x18, local copies, waits for them, and re-layouts: 5.94 us -> 7.79 us
  transfers between devices with their start and end apart: 8 -> 0, of which waited for: 6 -> 0; matrix products, arithmetic and copies ran while one was open for 9% -> 0% of each run, Pallas kernels for 0% -> 0%
where the time goes in v1:
time: 61.5 us; the launch traced here: 61 us
  Pallas kernels  50 us (81%)
  local copies, waits for them, and re-layouts  7.79 us (13%)
  other arithmetic  2.54 us (4%)
  between operations  0.66 us (1%)
    pallas_call x1, Pallas kernels, local_fast(): pl.pallas_call(functools.partial(kernel, chips), out_shape=(jax.ShapeDtyp...  50 us
    unnamed x18, local copies, waits for them, and re-layouts  7.79 us

profile of v1, /device:TPU:0, one launch (start us, length us, event | category | flops | bytes accessed | tf_op | source)
XLA Modules:
  0.0 61.0 jit_solution(10555484466527431446)
XLA Ops:
  0.6 0.0 copy-start.8
  0.6 0.8 %multiply_bitcast_fusion.1.filt_ref = f32[64,128]{1,0:T(8,128)S(1)} fusion(f32[128,64]{0,1:T(8,128)} %param.13), kind=kLoop, calls=%fused_computation.5 | loop fusion | flops 8192 | bytes 65536 | tf_op jit(solution)/shard_map/transpose | solution.py:469
  1.4 0.0 copy-done.8
  1.4 0.0 copy-start
  1.4 0.9 %copy-done = bf16[128,1024]{1,0:T(8,128)(2,1)S(1)} copy-done((bf16[128,1024]{1,0:T(8,128)(2,1)S(1)}, bf16[128,1024]{1,0:T(8,128)(2,1)}, u32[]{:S(2)}) %copy-start) | copy-done | bytes 262168
  2.4 0.0 copy-start.1
  2.4 0.9 %copy-done.1 = bf16[128,1024]{1,0:T(8,128)(2,1)S(1)} copy-done((bf16[128,1024]{1,0:T(8,128)(2,1)S(1)}, bf16[128,1024]{1,0:T(8,128)(2,1)}, u32[]{:S(2)}) %copy-start.1) | copy-done | bytes 262168
  3.3 0.0 copy-start.2
  3.3 0.9 %copy-done.2 = bf16[128,1024]{1,0:T(8,128)(2,1)S(1)} copy-done((bf16[128,1024]{1,0:T(8,128)(2,1)S(1)}, bf16[128,1024]{1,0:T(8,128)(2,1)}, u32[]{:S(2)}) %copy-start.2) | copy-done | bytes 262168
  4.3 0.0 copy-start.3
  4.3 0.9 %copy-done.3 = bf16[128,1024]{1,0:T(8,128)(2,1)S(1)} copy-done((bf16[128,1024]{1,0:T(8,128)(2,1)S(1)}, bf16[128,1024]{1,0:T(8,128)(2,1)}, u32[]{:S(2)}) %copy-start.3) | copy-done | bytes 262168
  5.2 0.0 copy-start.4
  5.2 1.0 %copy-done.4 = bf16[512,512]{1,0:T(8,128)(2,1)S(1)} copy-done((bf16[512,512]{1,0:T(8,128)(2,1)S(1)}, bf16[512,512]{1,0:T(8,128)(2,1)}, u32[]{:S(2)}) %copy-start.4) | copy-done | bytes 524312
  6.3 0.0 copy-start.5
  6.3 1.0 %copy-done.5 = bf16[512,512]{1,0:T(8,128)(2,1)S(1)} copy-done((bf16[512,512]{1,0:T(8,128)(2,1)S(1)}, bf16[512,512]{1,0:T(8,128)(2,1)}, u32[]{:S(2)}) %copy-start.5) | copy-done | bytes 524312
  7.3 0.0 copy-start.6
  7.3 0.9 %copy-done.6 = bf16[256,512]{1,0:T(8,128)(2,1)S(1)} copy-done((bf16[256,512]{1,0:T(8,128)(2,1)S(1)}, bf16[256,512]{1,0:T(8,128)(2,1)}, u32[]{:S(2)}) %copy-start.6) | copy-done | bytes 262168
  8.3 0.0 copy-start.7
  8.3 0.9 %copy-done.7 = bf16[256,512]{1,0:T(8,128)(2,1)S(1)} copy-done((bf16[256,512]{1,0:T(8,128)(2,1)S(1)}, bf16[256,512]{1,0:T(8,128)(2,1)}, u32[]{:S(2)}) %copy-start.7) | copy-done | bytes 262168
  9.2 50.0 %ring_conv.1 = (f32[128,1024]{1,0:T(8,128)S(1)}, f32[128,1024]{1,0:T(8,128)S(1)}, f32[64,128]{1,0:T(8,128)S(1)}) custom-call(bf16[128,1024]{1,0:T(8,128)(2,1)S(1)} %copy-done, bf16[128,1024]{1,0:T(8,128)(2,1)S(1)} %copy-done.1, bf16[128,1024]{1,0:T(8,128)(2,1)S(1)} %copy-done.2, bf16[128,1024]{1,0:T(8,128)(2,1)S(1)} %copy-done.3, ...), custom_call_target="tpu_custom_call" | custom-call | flops 10000000000 | bytes 8388608 | tf_op jit(solution)/shard_map/ring_conv/pallas_call | solution.py:455
  59.2 1.2 %multiply_convert_fusion = (bf16[128,1024]{1,0:T(8,128)(2,1)}, bf16[128,1024]{1,0:T(8,128)(2,1)}, bf16[128,1024]{1,0:T(8,128)(2,1)}, bf16[128,1024]{1,0:T(8,128)(2,1)}) fusion(f32[128,1024]{1,0:T(8,128)S(1)} %get-tuple-element.9, bf16[128,1024]{1,0:T(8,128)(2,1)S(1)} %copy-done.1, bf16[128,1024]{1,0:T(8,128)(2,1)S(1)} %copy-done.2, ...), kind=kLoop, calls=%fused_computation | loop fusion | flops 1572864 | bytes 3145728 | tf_op jit(solution)/shard_map/convert_element_type | solution.py:473
  60.4 0.6 %multiply_bitcast_fusion = f32[128,64]{0,1:T(8,128)} fusion(f32[64,128]{1,0:T(8,128)S(1)} %get-tuple-element.10), kind=kLoop, calls=%fused_computation.4 | loop fusion | flops 8192 | bytes 65536 | tf_op jit(solution)/shard_map/mul | solution.py:474
Async XLA Ops:
  0.6 0.8 %copy-start.8 = (bf16[4,32,128]{2,1,0:T(8,128)(2,1)S(1)}, bf16[4,32,128]{2,1,0:T(8,128)(2,1)}, u32[]{:S(2)}) copy-start(bf16[4,32,128]{2,1,0:T(8,128)(2,1)} %constant.16.clone.spread_ref) | copy-start | bytes 98308
  1.4 1.0 %copy-start = (bf16[128,1024]{1,0:T(8,128)(2,1)S(1)}, bf16[128,1024]{1,0:T(8,128)(2,1)}, u32[]{:S(2)}) copy-start(bf16[128,1024]{1,0:T(8,128)(2,1)} %q_ref.1) | copy-start | bytes 786436
  2.4 0.9 %copy-start.1 = (bf16[128,1024]{1,0:T(8,128)(2,1)S(1)}, bf16[128,1024]{1,0:T(8,128)(2,1)}, u32[]{:S(2)}) copy-start(bf16[128,1024]{1,0:T(8,128)(2,1)} %k_ref.1) | copy-start | bytes 786436
  3.3 0.9 %copy-start.2 = (bf16[128,1024]{1,0:T(8,128)(2,1)S(1)}, bf16[128,1024]{1,0:T(8,128)(2,1)}, u32[]{:S(2)}) copy-start(bf16[128,1024]{1,0:T(8,128)(2,1)} %v_ref.1) | copy-start | bytes 786436
  4.3 0.9 %copy-start.3 = (bf16[128,1024]{1,0:T(8,128)(2,1)S(1)}, bf16[128,1024]{1,0:T(8,128)(2,1)}, u32[]{:S(2)}) copy-start(bf16[128,1024]{1,0:T(8,128)(2,1)} %go_ref.1) | copy-start | bytes 786436
  5.2 1.0 %copy-start.4 = (bf16[512,512]{1,0:T(8,128)(2,1)S(1)}, bf16[512,512]{1,0:T(8,128)(2,1)}, u32[]{:S(2)}) copy-start(bf16[512,512]{1,0:T(8,128)(2,1)} %constant.13.clone.fwd_lo) | copy-start | bytes 1572868
  6.3 1.0 %copy-start.5 = (bf16[512,512]{1,0:T(8,128)(2,1)S(1)}, bf16[512,512]{1,0:T(8,128)(2,1)}, u32[]{:S(2)}) copy-start(bf16[512,512]{1,0:T(8,128)(2,1)} %constant.12.clone.fwd_hi) | copy-start | bytes 1572868
  7.3 0.9 %copy-start.6 = (bf16[256,512]{1,0:T(8,128)(2,1)S(1)}, bf16[256,512]{1,0:T(8,128)(2,1)}, u32[]{:S(2)}) copy-start(bf16[256,512]{1,0:T(8,128)(2,1)} %constant.15.clone.inv_lo) | copy-start | bytes 786436
  8.3 0.9 %copy-start.7 = (bf16[256,512]{1,0:T(8,128)(2,1)S(1)}, bf16[256,512]{1,0:T(8,128)(2,1)}, u32[]{:S(2)}) copy-start(bf16[256,512]{1,0:T(8,128)(2,1)} %constant.14.clone.inv_hi) | copy-start | bytes 786436

commit v2 on v1

--- a/solution.py
+++ b/solution.py
@@ -164,10 +164,11 @@
     return dot(a[0], b[0], dims) + dot(a[0], b[1], dims) + dot(a[1], b[0], dims)
 
 
-def kernel(chips, q_ref, k_ref, v_ref, go_ref, filt_ref, fwd_hi, fwd_lo, inv_hi, inv_lo, spread_ref,
+def kernel(chips, q_hbm, k_hbm, v_hbm, go_hbm, filt_hbm, fwd_hi_hbm, fwd_lo_hbm, inv_hi_hbm, inv_lo_hbm, spread_hbm,
            conv_ref, gg_ref, gf_ref,
-           g_buf, r_buf, sg_buf, h_buf, h_spec, conv_acc, gg_acc, r_spec, c_spec, y_buf, x_buf, c_own, c_buf, f_buf,
-           f_send, f_recv, e_send, e_recv, g_send, g_recv, r_send, r_recv, y_send, y_recv, c_send, c_recv, p_send, p_recv):
+           q_ref, k_ref, v_ref, go_ref, filt_ref, fwd_hi, fwd_lo, inv_hi, inv_lo, spread_ref,
+           g_buf, r_buf, sg_buf, h_buf, h_spec, conv_acc, gg_acc, r_spec, r_next, part_acc, part_buf, c_spec, y_buf, x_buf, c_own, c_buf, f_buf,
+           f_send, f_recv, e_send, e_recv, g_send, g_recv, r_send, r_recv, y_send, y_recv, c_send, c_recv, load_sem, p_send, p_recv):
     groups = 2 * chips
     rows = q_ref.shape[0]
     half = q_ref.shape[1] // 2
@@ -191,11 +192,20 @@
     my_rows = pl.ds(pl.multiple_of(c * rows, rows), rows)
     its_rows = pl.ds(pl.multiple_of((1 - c) * rows, rows), rows)
 
+    loads = [pltpu.make_async_copy(src, dst, load_sem.at[i]) for i, (src, dst) in enumerate((
+        (k_hbm, k_ref), (v_hbm, v_ref), (go_hbm, go_ref), (q_hbm, q_ref), (filt_hbm, filt_ref),
+        (fwd_hi_hbm, fwd_hi), (fwd_lo_hbm, fwd_lo), (spread_hbm, spread_ref), (inv_hi_hbm, inv_hi),
+        (inv_lo_hbm, inv_lo)))]
+    for load in loads:
+        load.start()
+
     barrier = pltpu.get_barrier_semaphore()
     for d in range(1, groups):
         pl.semaphore_signal(barrier, inc=1, device_id={"context": (me + d) % groups},
                             device_id_type=pl.DeviceIdType.MESH)
     pl.semaphore_wait(barrier, groups - 1)
+    for load in loads[:5]:
+        load.wait()
 
     def swap(which, j):
         buf = g_buf if which == 0 else r_buf
@@ -251,6 +261,8 @@
 
     lax.fori_loop(0, chunks, first_sends, 0)
 
+    for load in loads[5:]:
+        load.wait()
     for d in range(1, groups):
         filter_copy(d).wait_recv()
 
@@ -283,8 +295,8 @@
         ar, ai, br, bi = a[:block], a[block:], b[:block], b[block:]
         return jnp.concatenate([ar * br - ai * bi, ar * bi + ai * br], axis=0)
 
-    def add_corr(m, j, g):
-        prod = halves(conj_times(g, r_spec[j]))
+    def add_corr(m, j, g, r):
+        prod = halves(conj_times(g, r))
         c_spec[m] += dot(spread_ref[j], prod[0], NT) + dot(spread_ref[j], prod[1], NT)
 
     def own_step(j, carry):
@@ -293,7 +305,7 @@
         gg_acc[j] = conj_times(h_spec[0, j], r)
         g = spectrum(g_buf[0, j])
         conv_acc[j] = times(h_spec[0, j], g)
-        add_corr(0, j, g)
+        add_corr(0, j, g, r)
         return carry
 
     lax.fori_loop(0, chunks, own_step, 0)
@@ -302,35 +314,70 @@
         return remote(y_buf.at[which, j, its_rows, :], x_buf.at[which, j],
                       y_send.at[which, j], y_recv.at[which, j], partner)
 
+    def inverse(spec):
+        return dot3((inv_hi[...], inv_lo[...]), halves(spec))
+
+    def part_copy(which, j):
+        if which == 0:
+            return remote(part_buf.at[0, j], g_buf.at[2, j], g_send.at[1, j], g_recv.at[1, j], right)
+        return remote(part_buf.at[1, j], r_buf.at[2, j], r_send.at[1, j], r_recv.at[1, j], left)
+
     def finish(j):
-        for which, acc, out in ((0, conv_acc, conv_ref), (1, gg_acc, gg_ref)):
-            y_buf[which, j] = dot3((inv_hi[...], inv_lo[...]), halves(acc[j]))
+        for which, near, end in ((0, chips - 2, chips - 1), (1, 1, 0)):
+            @pl.when(z == near)
+            def _():
+                part_buf[which, j] = inverse(part_acc[which, j])
+                part_copy(which, j).start()
+
+        for which, acc, out, end in ((0, conv_acc, conv_ref, chips - 1), (1, gg_acc, gg_ref, 0)):
+            y_buf[which, j] = inverse(acc[j])
+
+            @pl.when(z == end)
+            def _():
+                part_copy(which, j).wait_recv()
+                y_buf[which, j] += (g_buf if which == 0 else r_buf)[2, j]
+
             y_copy(which, j).start()
             out[:, columns(c, j)] = y_buf[which, j, my_rows, :]
 
-    for s in range(chips - 1):
+    last_step = chips - 3
+    for s in range(last_step + 1):
         def step(j, carry):
-            @pl.when(z - 1 - s >= 0)
+            @pl.when((z + 1 + s < chips) & ((z >= 1) | (s == 0)))
+            def _():
+                r_copy(s, j).wait_recv()
+                if s < last_step:
+                    @pl.when(z >= 2)
+                    def _():
+                        r_copy(s + 1, j).start()
+                r = spectrum(r_buf[s + 1, j])
+                gg_acc[j] += conj_times(h_spec[s + 1, j], r)
+                if s == 0:
+                    r_next[j] = r
+
+                @pl.when(z == 1)
+                def _():
+                    term = conj_times(h_spec[s + 2, j], r)
+                    part_acc[1, j] = term if s == 0 else part_acc[1, j] + term
+
+            @pl.when((z - 1 - s >= 0) & ((z <= chips - 2) | (s == 0)))
             def _():
                 g_copy(s, j).wait_recv()
-                if s < chips - 2:
-                    @pl.when(z + 1 < chips)
+                if s < last_step:
+                    @pl.when(z <= chips - 3)
                     def _():
                         g_copy(s + 1, j).start()
                 g = spectrum(g_buf[s + 1, j])
                 conv_acc[j] += times(h_spec[s + 1, j], g)
-                add_corr(s + 1, j, g)
-
-            @pl.when(z + 1 + s < chips)
-            def _():
-                r_copy(s, j).wait_recv()
-                if s < chips - 2:
-                    @pl.when(z >= 1)
-                    def _():
-                        r_copy(s + 1, j).start()
-                gg_acc[j] += conj_times(h_spec[s + 1, j], spectrum(r_buf[s + 1, j]))
-
-            if s == chips - 2:
+                add_corr(s + 1, j, g, r_spec[j])
+
+                @pl.when(z == chips - 2)
+                def _():
+                    term = times(h_spec[s + 2, j], g)
+                    part_acc[0, j] = term if s == 0 else part_acc[0, j] + term
+                    add_corr(s + 2, j, g, r_next[j])
+
+            if s == last_step:
                 finish(j)
             return carry
 
@@ -344,19 +391,24 @@
     def c_copy(n):
         return remote(c_own.at[n], c_buf.at[z], c_send.at[n], c_recv.at[z], n * 2 + c)
 
+    my_reach = jnp.where(z == chips - 2, chips - 1, jnp.where(z == chips - 1, 1, z))
+
+    def reach(chip):
+        return {chips - 2: chips - 1, chips - 1: 1}.get(chip, chip)
+
     for n in range(chips):
-        @pl.when(n <= z)
+        @pl.when((n <= my_reach) | (n == z))
         def _():
             total = lag_block(n)
             c_own[n, 0] = total[:, :rows]
             c_own[n, 1] = total[:, rows:]
 
-        @pl.when(n < z)
+        @pl.when((n <= my_reach) & (n != z))
         def _():
             c_copy(n).start()
 
     for i in range(1, chips):
-        @pl.when(i > z)
+        @pl.when((z <= reach(i)) & (i != z))
         def _():
             remote(c_own.at[0], c_buf.at[i], c_send.at[0], c_recv.at[i], partner).wait_recv()
             c_own[z] += c_buf[i]
@@ -376,8 +428,8 @@
     gf_ref[pl.ds(pl.multiple_of((1 - c) * nf, nf), nf), :] = f_buf[...]
 
     last.wait_send()
-    for n in range(chips - 1):
-        @pl.when(n < z)
+    for n in range(chips):
+        @pl.when((n <= my_reach) & (n != z))
         def _():
             c_copy(n).wait_send()
     for d in range(1, groups):
@@ -387,14 +439,19 @@
         for which in range(2):
             swap(which, j).wait_send()
             y_copy(which, j).wait_send()
-        for s in range(chips - 1):
-            @pl.when((z - s >= 0) & (z + 1 < chips))
+        for s in range(last_step + 1):
+            @pl.when((z - s >= 0) & (z + 1 < (chips if s == 0 else chips - 1)))
             def _():
                 g_copy(s, j).wait_send()
 
-            @pl.when((z + s < chips) & (z >= 1))
+            @pl.when((z + s < chips) & (z >= (1 if s == 0 else 2)))
             def _():
                 r_copy(s, j).wait_send()
+
+        for which, near in ((0, chips - 2), (1, 1)):
+            @pl.when(z == near)
+            def _():
+                part_copy(which, j).wait_send()
         return carry
 
     lax.fori_loop(0, chunks, drain, 0)
@@ -412,6 +469,9 @@
         (chunks, 2 * block, LANES),
         (chunks, 2 * block, LANES),
         (chunks, 2 * block, LANES),
+        (chunks, 2 * block, LANES),
+        (2, chunks, 2 * block, LANES),
+        (2, chunks, block, LANES),
         (chips + 1, nf, 2 * block),
         (2, chunks, block, LANES),
         (2, chunks, rows, LANES),
@@ -423,9 +483,14 @@
     sems = [
         (2 * chips,), (2 * chips,), (2, chunks), (2, chunks), (steps, chunks), (steps, chunks),
         (steps, chunks), (steps, chunks), (2, chunks), (2, chunks), (chips,), (chips,),
+        (10,),
     ]
     used = sum(4 * math.prod(shape) for shape in memory)
-    specs = [pltpu.VMEM(shape, f32) for shape in memory]
+    held = [((rows, 2 * half), jnp.bfloat16)] * 4 + [((2 * nf, rows), f32)]
+    held += [((2 * block, 2 * block), jnp.bfloat16)] * 2 + [((block, 2 * block), jnp.bfloat16)] * 2
+    held += [((chunks, nf, LANES), jnp.bfloat16)]
+    specs = [pltpu.VMEM(shape, kind) for shape, kind in held]
+    specs += [pltpu.VMEM(shape, f32) for shape in memory]
     specs += [pltpu.SemaphoreType.DMA(shape) for shape in sems]
     specs += [pltpu.SemaphoreType.DMA, pltpu.SemaphoreType.DMA]
     return used, specs
@@ -434,7 +499,7 @@
 def fits(chips, rows, width, filters):
     used, _ = scratch(chips, rows, width // 2, filters // 2)
     aligned = rows % LANES == 0 and width % (2 * LANES) == 0 and filters % 16 == 0
-    return aligned and chips >= 2 and used <= VMEM_BUDGET // 2
+    return aligned and chips >= 3 and used <= VMEM_BUDGET // 2
 
 
 def local_fast(query_gate, key_gate, value_in, filter_raw, grad_out):
@@ -459,7 +524,7 @@
             jax.ShapeDtypeStruct((rows, width), jnp.float32),
             jax.ShapeDtypeStruct((filters, rows), jnp.float32),
         ),
-        in_specs=[vmem] * 10,
+        in_specs=[pl.BlockSpec(memory_space=pltpu.HBM)] * 10,
         out_specs=(vmem,) * 3,
         scratch_shapes=scratches,
         compiler_params=pltpu.CompilerParams(

time: 61.5 us -> 56.5 us (0.919)
  Pallas kernels: 50 us -> 45 us
    pallas_call x1, Pallas kernels: 50 us -> 45 us  [local_fast(): pl.pallas_call(functools.partial(kernel, chips), out_shape=(jax.ShapeDtyp...]
where the time goes in v2:
time: 56.5 us; the launch traced here: 56 us
  Pallas kernels  45 us (80%)
  local copies, waits for them, and re-layouts  7.79 us (14%)
  other arithmetic  2.54 us (4%)
  between operations  0.66 us (1%)
    pallas_call x1, Pallas kernels, local_fast(): pl.pallas_call(functools.partial(kernel, chips), out_shape=(jax.ShapeDtyp...  45 us
    unnamed x18, local copies, waits for them, and re-layouts  7.79 us
    convert_element_type x1, other arithmetic, local_fast(): (grad_gated * key_gate.astype(jnp.float32)).astype(jnp.bfloat16)  1.16 us

profile of v2, /device:TPU:0, one launch (start us, length us, event | category | flops | bytes accessed | tf_op | source)
XLA Modules:
  0.0 56.0 jit_solution(6781519429259655102)
XLA Ops:
  0.6 0.0 copy-start.8
  0.6 0.8 %multiply_bitcast_fusion.1.filt_hbm = f32[64,128]{1,0:T(8,128)S(1)} fusion(f32[128,64]{0,1:T(8,128)} %param.13), kind=kLoop, calls=%fused_computation.5 | loop fusion | flops 8192 | bytes 65536 | tf_op jit(solution)/shard_map/transpose | solution.py:534
  1.4 0.0 copy-done.8
  1.4 0.0 copy-start
  1.4 0.9 %copy-done = bf16[128,1024]{1,0:T(8,128)(2,1)S(1)} copy-done((bf16[128,1024]{1,0:T(8,128)(2,1)S(1)}, bf16[128,1024]{1,0:T(8,128)(2,1)}, u32[]{:S(2)}) %copy-start) | copy-done | bytes 262168
  2.4 0.0 copy-start.1
  2.4 0.9 %copy-done.1 = bf16[128,1024]{1,0:T(8,128)(2,1)S(1)} copy-done((bf16[128,1024]{1,0:T(8,128)(2,1)S(1)}, bf16[128,1024]{1,0:T(8,128)(2,1)}, u32[]{:S(2)}) %copy-start.1) | copy-done | bytes 262168
  3.3 0.0 copy-start.2
  3.3 0.9 %copy-done.2 = bf16[128,1024]{1,0:T(8,128)(2,1)S(1)} copy-done((bf16[128,1024]{1,0:T(8,128)(2,1)S(1)}, bf16[128,1024]{1,0:T(8,128)(2,1)}, u32[]{:S(2)}) %copy-start.2) | copy-done | bytes 262168
  4.3 0.0 copy-start.3
  4.3 0.9 %copy-done.3 = bf16[128,1024]{1,0:T(8,128)(2,1)S(1)} copy-done((bf16[128,1024]{1,0:T(8,128)(2,1)S(1)}, bf16[128,1024]{1,0:T(8,128)(2,1)}, u32[]{:S(2)}) %copy-start.3) | copy-done | bytes 262168
  5.2 0.0 copy-start.4
  5.2 1.0 %copy-done.4 = bf16[512,512]{1,0:T(8,128)(2,1)S(1)} copy-done((bf16[512,512]{1,0:T(8,128)(2,1)S(1)}, bf16[512,512]{1,0:T(8,128)(2,1)}, u32[]{:S(2)}) %copy-start.4) | copy-done | bytes 524312
  6.3 0.0 copy-start.5
  6.3 1.0 %copy-done.5 = bf16[512,512]{1,0:T(8,128)(2,1)S(1)} copy-done((bf16[512,512]{1,0:T(8,128)(2,1)S(1)}, bf16[512,512]{1,0:T(8,128)(2,1)}, u32[]{:S(2)}) %copy-start.5) | copy-done | bytes 524312
  7.3 0.0 copy-start.6
  7.3 0.9 %copy-done.6 = bf16[256,512]{1,0:T(8,128)(2,1)S(1)} copy-done((bf16[256,512]{1,0:T(8,128)(2,1)S(1)}, bf16[256,512]{1,0:T(8,128)(2,1)}, u32[]{:S(2)}) %copy-start.6) | copy-done | bytes 262168
  8.3 0.0 copy-start.7
  8.3 0.9 %copy-done.7 = bf16[256,512]{1,0:T(8,128)(2,1)S(1)} copy-done((bf16[256,512]{1,0:T(8,128)(2,1)S(1)}, bf16[256,512]{1,0:T(8,128)(2,1)}, u32[]{:S(2)}) %copy-start.7) | copy-done | bytes 262168
  9.2 45.0 %ring_conv.1 = (f32[128,1024]{1,0:T(8,128)S(1)}, f32[128,1024]{1,0:T(8,128)S(1)}, f32[64,128]{1,0:T(8,128)S(1)}) custom-call(bf16[128,1024]{1,0:T(8,128)(2,1)S(1)} %copy-done, bf16[128,1024]{1,0:T(8,128)(2,1)S(1)} %copy-done.1, bf16[128,1024]{1,0:T(8,128)(2,1)S(1)} %copy-done.2, bf16[128,1024]{1,0:T(8,128)(2,1)S(1)} %copy-done.3, ...), custom_call_target="tpu_custom_call" | custom-call | flops 10000000000 | bytes 8388608 | tf_op jit(solution)/shard_map/ring_conv/pallas_call | solution.py:520
  54.2 1.2 %multiply_convert_fusion = (bf16[128,1024]{1,0:T(8,128)(2,1)}, bf16[128,1024]{1,0:T(8,128)(2,1)}, bf16[128,1024]{1,0:T(8,128)(2,1)}, bf16[128,1024]{1,0:T(8,128)(2,1)}) fusion(f32[128,1024]{1,0:T(8,128)S(1)} %get-tuple-element.9, bf16[128,1024]{1,0:T(8,128)(2,1)S(1)} %copy-done.1, bf16[128,1024]{1,0:T(8,128)(2,1)S(1)} %copy-done.2, ...), kind=kLoop, calls=%fused_computation | loop fusion | flops 1572864 | bytes 3145728 | tf_op jit(solution)/shard_map/convert_element_type | solution.py:538
  55.4 0.6 %multiply_bitcast_fusion = f32[128,64]{0,1:T(8,128)} fusion(f32[64,128]{1,0:T(8,128)S(1)} %get-tuple-element.10), kind=kLoop, calls=%fused_computation.4 | loop fusion | flops 8192 | bytes 65536 | tf_op jit(solution)/shard_map/mul | solution.py:539
Async XLA Ops:
  0.6 0.8 %copy-start.8 = (bf16[4,32,128]{2,1,0:T(8,128)(2,1)S(1)}, bf16[4,32,128]{2,1,0:T(8,128)(2,1)}, u32[]{:S(2)}) copy-start(bf16[4,32,128]{2,1,0:T(8,128)(2,1)} %constant.16.clone.spread_hbm) | copy-start | bytes 98308
  1.4 1.0 %copy-start = (bf16[128,1024]{1,0:T(8,128)(2,1)S(1)}, bf16[128,1024]{1,0:T(8,128)(2,1)}, u32[]{:S(2)}) copy-start(bf16[128,1024]{1,0:T(8,128)(2,1)} %q_hbm.1) | copy-start | bytes 786436
  2.4 0.9 %copy-start.1 = (bf16[128,1024]{1,0:T(8,128)(2,1)S(1)}, bf16[128,1024]{1,0:T(8,128)(2,1)}, u32[]{:S(2)}) copy-start(bf16[128,1024]{1,0:T(8,128)(2,1)} %k_hbm.1) | copy-start | bytes 786436
  3.3 0.9 %copy-start.2 = (bf16[128,1024]{1,0:T(8,128)(2,1)S(1)}, bf16[128,1024]{1,0:T(8,128)(2,1)}, u32[]{:S(2)}) copy-start(bf16[128,1024]{1,0:T(8,128)(2,1)} %v_hbm.1) | copy-start | bytes 786436
  4.3 0.9 %copy-start.3 = (bf16[128,1024]{1,0:T(8,128)(2,1)S(1)}, bf16[128,1024]{1,0:T(8,128)(2,1)}, u32[]{:S(2)}) copy-start(bf16[128,1024]{1,0:T(8,128)(2,1)} %go_hbm.1) | copy-start | bytes 786436
  5.2 1.0 %copy-start.4 = (bf16[512,512]{1,0:T(8,128)(2,1)S(1)}, bf16[512,512]{1,0:T(8,128)(2,1)}, u32[]{:S(2)}) copy-start(bf16[512,512]{1,0:T(8,128)(2,1)} %constant.13.clone.fwd_lo_hbm) | copy-start | bytes 1572868
  6.3 1.0 %copy-start.5 = (bf16[512,512]{1,0:T(8,128)(2,1)S(1)}, bf16[512,512]{1,0:T(8,128)(2,1)}, u32[]{:S(2)}) copy-start(bf16[512,512]{1,0:T(8,128)(2,1)} %constant.12.clone.fwd_hi_hbm) | copy-start | bytes 1572868
  7.3 0.9 %copy-start.6 = (bf16[256,512]{1,0:T(8,128)(2,1)S(1)}, bf16[256,512]{1,0:T(8,128)(2,1)}, u32[]{:S(2)}) copy-start(bf16[256,512]{1,0:T(8,128)(2,1)} %constant.15.clone.inv_lo_hbm) | copy-start | bytes 786436
  8.3 0.9 %copy-start.7 = (bf16[256,512]{1,0:T(8,128)(2,1)S(1)}, bf16[256,512]{1,0:T(8,128)(2,1)}, u32[]{:S(2)}) copy-start(bf16[256,512]{1,0:T(8,128)(2,1)} %constant.14.clone.inv_hi_hbm) | copy-start | bytes 786436

commit v3 on v2

--- a/solution.py
+++ b/solution.py
@@ -130,6 +130,7 @@
 
 LANES = 128
 VMEM_BUDGET = 40 * 2**20
+VMEM_LIMIT = 60 * 2**20
 
 
 def halves(table):
@@ -154,19 +155,22 @@
 
 NN = (((1,), (0,)), ((), ()))
 NT = (((1,), (1,)), ((), ()))
+TN = (((0,), (0,)), ((), ()))
 
 
 def dot(a, b, dims=NN):
     return lax.dot_general(a, b, dims, preferred_element_type=jnp.float32)
 
 
-def dot3(a, b, dims=NN):
-    return dot(a[0], b[0], dims) + dot(a[0], b[1], dims) + dot(a[1], b[0], dims)
-
-
-def kernel(chips, q_hbm, k_hbm, v_hbm, go_hbm, filt_hbm, fwd_hi_hbm, fwd_lo_hbm, inv_hi_hbm, inv_lo_hbm, spread_hbm,
+def dot3(a, b):
+    count = b[0].shape[1]
+    wide = dot(a[0], jnp.concatenate(b, axis=1))
+    return wide[:, :count] + wide[:, count:] + dot(a[1], b[0])
+
+
+def kernel(chips, q_hbm, k_hbm, v_hbm, go_hbm, filt_hbm, fwd_hi_hbm, fwd_lo_hbm, inv_hi_hbm, inv_lo_hbm, spread_hbm, gather_hbm,
            conv_ref, gg_ref, gf_ref,
-           q_ref, k_ref, v_ref, go_ref, filt_ref, fwd_hi, fwd_lo, inv_hi, inv_lo, spread_ref,
+           q_ref, k_ref, v_ref, go_ref, filt_ref, fwd_hi, fwd_lo, inv_hi, inv_lo, spread_ref, gather_ref,
            g_buf, r_buf, sg_buf, h_buf, h_spec, conv_acc, gg_acc, r_spec, r_next, part_acc, part_buf, c_spec, y_buf, x_buf, c_own, c_buf, f_buf,
            f_send, f_recv, e_send, e_recv, g_send, g_recv, r_send, r_recv, y_send, y_recv, c_send, c_recv, load_sem, p_send, p_recv):
     groups = 2 * chips
@@ -194,7 +198,7 @@
 
     loads = [pltpu.make_async_copy(src, dst, load_sem.at[i]) for i, (src, dst) in enumerate((
         (k_hbm, k_ref), (v_hbm, v_ref), (go_hbm, go_ref), (q_hbm, q_ref), (filt_hbm, filt_ref),
-        (fwd_hi_hbm, fwd_hi), (fwd_lo_hbm, fwd_lo), (spread_hbm, spread_ref), (inv_hi_hbm, inv_hi),
+        (fwd_hi_hbm, fwd_hi), (fwd_lo_hbm, fwd_lo), (spread_hbm, spread_ref), (gather_hbm, gather_ref), (inv_hi_hbm, inv_hi),
         (inv_lo_hbm, inv_lo)))]
     for load in loads:
         load.start()
@@ -266,22 +270,24 @@
     for d in range(1, groups):
         filter_copy(d).wait_recv()
 
-    def lag_spectrum(m, carry):
-        late = jnp.concatenate([h_buf[m, 0], h_buf[m, 1]], axis=1)
-        before = jnp.maximum(m - 1, 0)
-        early = jnp.concatenate([h_buf[before, 0], h_buf[before, 1]], axis=1)
-        early = early * (m > 0).astype(jnp.float32)
-        window = halves(jnp.concatenate([early, late], axis=1))
-        spec = halves(dot3((fwd_hi[...], fwd_lo[...]), window, NT))
-
-        def widen(j, inner):
-            h_spec[m, j] = dot(spec[0], spread_ref[j]) + dot(spec[1], spread_ref[j])
-            return inner
-
-        lax.fori_loop(0, chunks, widen, 0)
-        return carry
-
-    lax.fori_loop(0, chips, lag_spectrum, 0)
+    lags = chips * nf
+    taps = halves(jnp.concatenate(
+        [h_buf[:, 0].reshape(lags, rows), h_buf[:, 1].reshape(lags, rows)], axis=1))
+    wide = dot(fwd_hi[:, block:], jnp.concatenate(taps, axis=0), NT)
+    spec = wide[:, :lags] + wide[:, lags:] + dot(fwd_lo[:, block:], taps[0], NT)
+    early = jnp.concatenate([jnp.zeros((2 * block, nf), jnp.float32), spec[:, :lags - nf]], axis=1)
+    sign = (1 - 2 * (lax.broadcasted_iota(jnp.int32, (block, lags), 0) % 2)).astype(jnp.float32)
+    spec = jnp.concatenate(
+        [spec[:block] - sign * early[block:], spec[block:] + sign * early[:block]], axis=0)
+    spec = jnp.concatenate(halves(spec), axis=1)
+
+    def widen(m, carry):
+        full = dot(spec, spread_ref[m])
+        for j in range(chunks):
+            h_spec[m, j] = full[:, j * LANES:(j + 1) * LANES]
+        return carry
+
+    lax.fori_loop(0, chips, widen, 0)
     c_spec[...] = jnp.zeros_like(c_spec)
 
     def spectrum(signal):
@@ -296,8 +302,8 @@
         return jnp.concatenate([ar * br - ai * bi, ar * bi + ai * br], axis=0)
 
     def add_corr(m, j, g, r):
-        prod = halves(conj_times(g, r))
-        c_spec[m] += dot(spread_ref[j], prod[0], NT) + dot(spread_ref[j], prod[1], NT)
+        prod = jnp.concatenate(halves(conj_times(g, r)), axis=1)
+        c_spec[...] += dot(prod, gather_ref[m, j])
 
     def own_step(j, carry):
         r = spectrum(r_buf[0, j])
@@ -383,10 +389,12 @@
 
         lax.fori_loop(0, chunks, step, 0)
 
-    def lag_block(n):
-        here = dot3(halves(c_spec[n]), (fwd_hi[:, block:], fwd_lo[:, block:]))
-        after = dot3(halves(c_spec[n + 1]), (fwd_hi[:, :block], fwd_lo[:, :block]))
-        return (here + after) * (1.0 / block)
+    corr = halves(c_spec[...])
+    both = jnp.concatenate(corr, axis=1)
+    wide = dot(both, fwd_hi[...], TN)
+    turned = wide[:lags] + wide[lags:] + dot(corr[0], fwd_lo[...], TN)
+    below = jnp.concatenate([turned[nf:, :block], jnp.zeros((nf, block), jnp.float32)], axis=0)
+    sums = (turned[:, block:] + below) * (1.0 / block)
 
     def c_copy(n):
         return remote(c_own.at[n], c_buf.at[z], c_send.at[n], c_recv.at[z], n * 2 + c)
@@ -397,11 +405,8 @@
         return {chips - 2: chips - 1, chips - 1: 1}.get(chip, chip)
 
     for n in range(chips):
-        @pl.when((n <= my_reach) | (n == z))
-        def _():
-            total = lag_block(n)
-            c_own[n, 0] = total[:, :rows]
-            c_own[n, 1] = total[:, rows:]
+        c_own[n, 0] = sums[n * nf:(n + 1) * nf, :rows]
+        c_own[n, 1] = sums[n * nf:(n + 1) * nf, rows:]
 
         @pl.when((n <= my_reach) & (n != z))
         def _():
@@ -472,7 +477,7 @@
         (chunks, 2 * block, LANES),
         (2, chunks, 2 * block, LANES),
         (2, chunks, block, LANES),
-        (chips + 1, nf, 2 * block),
+        (2 * block, chips * nf),
         (2, chunks, block, LANES),
         (2, chunks, rows, LANES),
         (chips, 2, nf, rows),
@@ -483,12 +488,12 @@
     sems = [
         (2 * chips,), (2 * chips,), (2, chunks), (2, chunks), (steps, chunks), (steps, chunks),
         (steps, chunks), (steps, chunks), (2, chunks), (2, chunks), (chips,), (chips,),
-        (10,),
+        (11,),
     ]
     used = sum(4 * math.prod(shape) for shape in memory)
     held = [((rows, 2 * half), jnp.bfloat16)] * 4 + [((2 * nf, rows), f32)]
     held += [((2 * block, 2 * block), jnp.bfloat16)] * 2 + [((block, 2 * block), jnp.bfloat16)] * 2
-    held += [((chunks, nf, LANES), jnp.bfloat16)]
+    held += [((chips, 2 * chips * nf, half), jnp.bfloat16), ((chips, chunks, 2 * LANES, chips * nf), jnp.bfloat16)]
     specs = [pltpu.VMEM(shape, kind) for shape, kind in held]
     specs += [pltpu.VMEM(shape, f32) for shape in memory]
     specs += [pltpu.SemaphoreType.DMA(shape) for shape in sems]
@@ -498,7 +503,7 @@
 
 def fits(chips, rows, width, filters):
     used, _ = scratch(chips, rows, width // 2, filters // 2)
-    aligned = rows % LANES == 0 and width % (2 * LANES) == 0 and filters % 16 == 0
+    aligned = rows % LANES == 0 and chips * filters == 2 * LANES and width % (2 * LANES) == 0 and filters % 16 == 0
     return aligned and chips >= 3 and used <= VMEM_BUDGET // 2
 
 
@@ -513,8 +518,11 @@
     forward = tables(block)
     fwd = np_halves(forward)
     inv = np_halves(forward[:, block:].T / block)
-    spread = np.kron(np.eye(nf), np.ones((1, width // filters)))
-    spread = spread.reshape(nf, chunks, LANES).transpose(1, 0, 2).astype(jnp.bfloat16)
+    member = np.kron(np.eye(chips * nf), np.ones((1, width // filters)))
+    member = member.reshape(chips * nf, chips, half).transpose(1, 0, 2)
+    spread = np.tile(member, (1, 2, 1)).astype(jnp.bfloat16)
+    gather = member.reshape(chips, chips * nf, chunks, LANES).transpose(0, 2, 3, 1)
+    gather = np.tile(gather, (1, 1, 2, 1)).astype(jnp.bfloat16)
     _, scratches = scratch(chips, rows, half, nf)
     vmem = pl.BlockSpec(memory_space=pltpu.VMEM)
     conv, grad_gated, corr = pl.pallas_call(
@@ -524,14 +532,14 @@
             jax.ShapeDtypeStruct((rows, width), jnp.float32),
             jax.ShapeDtypeStruct((filters, rows), jnp.float32),
         ),
-        in_specs=[pl.BlockSpec(memory_space=pltpu.HBM)] * 10,
+        in_specs=[pl.BlockSpec(memory_space=pltpu.HBM)] * 11,
         out_specs=(vmem,) * 3,
         scratch_shapes=scratches,
         compiler_params=pltpu.CompilerParams(
-            collective_id=0, has_side_effects=True, vmem_limit_bytes=VMEM_BUDGET),
+            collective_id=0, has_side_effects=True, vmem_limit_bytes=VMEM_LIMIT),
         cost_estimate=pl.CostEstimate(flops=10**10, bytes_accessed=8 * 2**20, transcendentals=0),
         name="ring_conv",
-    )(query_gate, key_gate, value_in, grad_out, (filter_raw * scale).T, *fwd, *inv, spread)
+    )(query_gate, key_gate, value_in, grad_out, (filter_raw * scale).T, *fwd, *inv, spread, gather)
     output = (query_gate.astype(jnp.float32) * conv).astype(jnp.bfloat16)
     grad_query = (grad_out.astype(jnp.float32) * conv).astype(jnp.bfloat16)
     grad_key = (grad_gated * value_in.astype(jnp.float32)).astype(jnp.bfloat16)

time: 56.5 us -> 50.9 us (0.901)
  local copies, waits for them, and re-layouts: 7.79 us -> 0.02 us
  other arithmetic: 2.54 us -> 4.35 us
  Pallas kernels: 45 us -> 45.6 us
    unnamed x18 -> x10, local copies, waits for them, and re-layouts: 7.79 us -> 0.02 us
    convert_element_type x1, other arithmetic: 1.16 us -> 2.36 us  [local_fast(): (grad_gated * key_gate.astype(jnp.float32)).astype(jnp.bfloat16)]
    transpose x1, other arithmetic: 0.77 us -> 1.38 us  [local_fast(): conv, grad_gated, corr = pl.pallas_call(functools.partial(kernel, chips),...]
    pallas_call x1, Pallas kernels: 45 us -> 45.6 us  [local_fast(): pl.pallas_call(functools.partial(kernel, chips), out_shape=(jax.ShapeDtyp...]
where the time goes in v3:
time: 50.9 us; the launch traced here: 50.7 us
  Pallas kernels  45.6 us (90%)
  other arithmetic  4.35 us (9%)
  between operations  0.68 us (1%)
    pallas_call x1, Pallas kernels, local_fast(): pl.pallas_call(functools.partial(kernel, chips), out_shape=(jax.ShapeDtyp...  45.6 us
    convert_element_type x1, other arithmetic, local_fast(): (grad_gated * key_gate.astype(jnp.float32)).astype(jnp.bfloat16)  2.36 us
    transpose x1, other arithmetic, local_fast(): conv, grad_gated, corr = pl.pallas_call(functools.partial(kernel, chips),...  1.38 us

profile of v3, /device:TPU:0, one launch (start us, length us, event | category | flops | bytes accessed | tf_op | source)
XLA Modules:
  0.0 50.7 jit_solution(18005304850446360114)
XLA Ops:
  0.6 1.4 %multiply_bitcast_fusion.1.filt_hbm = f32[64,128]{1,0:T(8,128)} fusion(f32[128,64]{0,1:T(8,128)} %param.14), kind=kLoop, calls=%fused_computation.5 | loop fusion | flops 8192 | bytes 65536 | tf_op jit(solution)/shard_map/transpose | solution.py:542
  2.0 0.0 copy-start
  2.0 0.0 copy-start.1
  2.0 0.0 copy-start.2
  2.0 0.0 copy-start.3
  2.0 45.6 %ring_conv.1 = (f32[128,1024]{1,0:T(8,128)}, f32[128,1024]{1,0:T(8,128)}, f32[64,128]{1,0:T(8,128)}) custom-call(bf16[128,1024]{1,0:T(8,128)(2,1)} %q_hbm.1, bf16[128,1024]{1,0:T(8,128)(2,1)} %k_hbm.1, bf16[128,1024]{1,0:T(8,128)(2,1)} %v_hbm.1, bf16[128,1024]{1,0:T(8,128)(2,1)} %go_hbm.1, f32[64,128]{1,0:T(8,128)} %multiply_bitcast_fusion.1.filt_hbm, ...), custom_call_target="tpu_custom_call" | custom-call | flops 10000000000 | bytes 8388608 | tf_op jit(solution)/shard_map/ring_conv/pallas_call | solution.py:528
  47.6 0.0 copy-done
  47.6 0.0 copy-done.1
  47.7 0.0 copy-done.2
  47.7 0.0 copy-done.3
  47.7 0.0 copy-start.4
  47.7 2.4 %multiply_convert_fusion = (bf16[128,1024]{1,0:T(8,128)(2,1)}, bf16[128,1024]{1,0:T(8,128)(2,1)}, bf16[128,1024]{1,0:T(8,128)(2,1)}, bf16[128,1024]{1,0:T(8,128)(2,1)}) fusion(f32[128,1024]{1,0:T(8,128)} %get-tuple-element.9, bf16[128,1024]{1,0:T(8,128)(2,1)S(1)} %copy-done.1, bf16[128,1024]{1,0:T(8,128)(2,1)S(1)} %copy-done.2, ...), kind=kLoop, calls=%fused_computation | loop fusion | flops 1572864 | bytes 3145728 | tf_op jit(solution)/shard_map/convert_element_type | solution.py:546
  50.0 0.0 copy-done.4
  50.0 0.6 %multiply_bitcast_fusion = f32[128,64]{0,1:T(8,128)} fusion(f32[64,128]{1,0:T(8,128)S(1)} %copy-done.4), kind=kLoop, calls=%fused_computation.4 | loop fusion | flops 8192 | bytes 65536 | tf_op jit(solution)/shard_map/mul | solution.py:547
Async XLA Ops:
  2.0 45.6 %copy-start = (bf16[128,1024]{1,0:T(8,128)(2,1)S(1)}, bf16[128,1024]{1,0:T(8,128)(2,1)}, u32[]{:S(2)}) copy-start(bf16[128,1024]{1,0:T(8,128)(2,1)} %q_hbm.1) | copy-start | bytes 786436
  2.0 45.6 %copy-start.1 = (bf16[128,1024]{1,0:T(8,128)(2,1)S(1)}, bf16[128,1024]{1,0:T(8,128)(2,1)}, u32[]{:S(2)}) copy-start(bf16[128,1024]{1,0:T(8,128)(2,1)} %k_hbm.1) | copy-start | bytes 786436
  2.0 45.6 %copy-start.2 = (bf16[128,1024]{1,0:T(8,128)(2,1)S(1)}, bf16[128,1024]{1,0:T(8,128)(2,1)}, u32[]{:S(2)}) copy-start(bf16[128,1024]{1,0:T(8,128)(2,1)} %v_hbm.1) | copy-start | bytes 786436
  2.0 45.7 %copy-start.3 = (bf16[128,1024]{1,0:T(8,128)(2,1)S(1)}, bf16[128,1024]{1,0:T(8,128)(2,1)}, u32[]{:S(2)}) copy-start(bf16[128,1024]{1,0:T(8,128)(2,1)} %go_hbm.1) | copy-start | bytes 786436
  47.7 2.4 %copy-start.4 = (f32[64,128]{1,0:T(8,128)S(1)}, f32[64,128]{1,0:T(8,128)}, u32[]{:S(2)}) copy-start(f32[64,128]{1,0:T(8,128)} %get-tuple-element.10) | copy-start | bytes 98308

commit v4 on v3

--- a/solution.py
+++ b/solution.py
@@ -168,11 +168,11 @@
     return wide[:, :count] + wide[:, count:] + dot(a[1], b[0])
 
 
-def kernel(chips, q_hbm, k_hbm, v_hbm, go_hbm, filt_hbm, fwd_hi_hbm, fwd_lo_hbm, inv_hi_hbm, inv_lo_hbm, spread_hbm, gather_hbm,
+def kernel(chips, scale, q_hbm, k_hbm, v_hbm, go_hbm, filt_hbm, fwd_hi_hbm, fwd_lo_hbm, inv_hi_hbm, inv_lo_hbm, spread_hbm, gather_hbm,
            conv_ref, gg_ref, gf_ref,
            q_ref, k_ref, v_ref, go_ref, filt_ref, fwd_hi, fwd_lo, inv_hi, inv_lo, spread_ref, gather_ref,
-           g_buf, r_buf, sg_buf, h_buf, h_spec, conv_acc, gg_acc, r_spec, r_next, part_acc, part_buf, c_spec, y_buf, x_buf, c_own, c_buf, f_buf,
-           f_send, f_recv, e_send, e_recv, g_send, g_recv, r_send, r_recv, y_send, y_recv, c_send, c_recv, load_sem, p_send, p_recv):
+           g_buf, r_buf, sg_buf, h_buf, h_spec, conv_acc, gg_acc, r_spec, r_next, part_acc, part_buf, c_spec, y_buf, x_buf, c_own, c_buf, end_buf,
+           f_send, f_recv, e_send, e_recv, g_send, g_recv, r_send, r_recv, y_send, y_recv, c_send, c_recv, load_sem, o_send, o_recv, p_send, p_recv):
     groups = 2 * chips
     rows = q_ref.shape[0]
     half = q_ref.shape[1] // 2
@@ -207,24 +207,25 @@
     for d in range(1, groups):
         pl.semaphore_signal(barrier, inc=1, device_id={"context": (me + d) % groups},
                             device_id_type=pl.DeviceIdType.MESH)
-    pl.semaphore_wait(barrier, groups - 1)
-    for load in loads[:5]:
-        load.wait()
-
     def swap(which, j):
         buf = g_buf if which == 0 else r_buf
         return remote(sg_buf.at[which, j], buf.at[0, j, my_rows, :],
                       e_send.at[which, j], e_recv.at[which, j], partner)
 
-    def gate_out(j, carry):
+    for load in loads[:5]:
+        load.wait()
+
+    def gate(j, carry):
         cols = columns(1 - c, j)
         sg_buf[0, j] = k_ref[:, cols].astype(jnp.float32) * v_ref[:, cols].astype(jnp.float32)
-        swap(0, j).start()
         sg_buf[1, j] = go_ref[:, cols].astype(jnp.float32) * q_ref[:, cols].astype(jnp.float32)
-        swap(1, j).start()
+        cols = columns(c, j)
+        g_buf[0, j, my_rows, :] = k_ref[:, cols].astype(jnp.float32) * v_ref[:, cols].astype(jnp.float32)
+        r_buf[0, j, my_rows, :] = go_ref[:, cols].astype(jnp.float32) * q_ref[:, cols].astype(jnp.float32)
         return carry
 
-    lax.fori_loop(0, chunks, gate_out, 0)
+    lax.fori_loop(0, chunks, gate, 0)
+    pl.semaphore_wait(barrier, groups - 1)
 
     def filter_copy(d):
         target = (me + d) % groups
@@ -235,13 +236,18 @@
         filter_copy(d).start()
     h_buf[z, c] = filt_ref[pl.ds(pl.multiple_of(c * nf, nf), nf), :]
 
-    def gate_own(j, carry):
-        cols = columns(c, j)
-        g_buf[0, j, my_rows, :] = k_ref[:, cols].astype(jnp.float32) * v_ref[:, cols].astype(jnp.float32)
-        r_buf[0, j, my_rows, :] = go_ref[:, cols].astype(jnp.float32) * q_ref[:, cols].astype(jnp.float32)
-        return carry
-
-    lax.fori_loop(0, chunks, gate_own, 0)
+    def own_copy(which, other, j):
+        buf = g_buf if which == 0 else r_buf
+        near = partner if other else me
+        target = (near + 2) % groups if which == 0 else (near + groups - 2) % groups
+        return remote(sg_buf.at[which, j] if other else buf.at[0, j, my_rows, :], buf.at[1, j, my_rows, :],
+                      o_send.at[which, other, j], o_recv.at[which, c, j], target)
+
+    def own_wait(which, j):
+        buf = g_buf if which == 0 else r_buf
+        for core in range(2):
+            remote(sg_buf.at[which, j], buf.at[1, j, core * rows:(core + 1) * rows, :],
+                   o_send.at[which, 0, j], o_recv.at[which, core, j], partner).wait_recv()
 
     def g_copy(s, j):
         return remote(g_buf.at[s, j], g_buf.at[s + 1, j], g_send.at[s, j], g_recv.at[s, j], right)
@@ -250,17 +256,18 @@
         return remote(r_buf.at[s, j], r_buf.at[s + 1, j], r_send.at[s, j], r_recv.at[s, j], left)
 
     def first_sends(j, carry):
-        swap(0, j).wait_recv()
+        swap(0, j).start()
+        swap(1, j).start()
 
         @pl.when(z + 1 < chips)
         def _():
-            g_copy(0, j).start()
-
-        swap(1, j).wait_recv()
+            own_copy(0, 0, j).start()
+            own_copy(0, 1, j).start()
 
         @pl.when(z >= 1)
         def _():
-            r_copy(0, j).start()
+            own_copy(1, 0, j).start()
+            own_copy(1, 1, j).start()
         return carry
 
     lax.fori_loop(0, chunks, first_sends, 0)
@@ -272,7 +279,7 @@
 
     lags = chips * nf
     taps = halves(jnp.concatenate(
-        [h_buf[:, 0].reshape(lags, rows), h_buf[:, 1].reshape(lags, rows)], axis=1))
+        [h_buf[:, 0].reshape(lags, rows), h_buf[:, 1].reshape(lags, rows)], axis=1) * scale)
     wide = dot(fwd_hi[:, block:], jnp.concatenate(taps, axis=0), NT)
     spec = wide[:, :lags] + wide[:, lags:] + dot(fwd_lo[:, block:], taps[0], NT)
     early = jnp.concatenate([jnp.zeros((2 * block, nf), jnp.float32), spec[:, :lags - nf]], axis=1)
@@ -306,6 +313,8 @@
         c_spec[...] += dot(prod, gather_ref[m, j])
 
     def own_step(j, carry):
+        swap(0, j).wait_recv()
+        swap(1, j).wait_recv()
         r = spectrum(r_buf[0, j])
         r_spec[j] = r
         gg_acc[j] = conj_times(h_spec[0, j], r)
@@ -323,26 +332,21 @@
     def inverse(spec):
         return dot3((inv_hi[...], inv_lo[...]), halves(spec))
 
-    def part_copy(which, j):
-        if which == 0:
-            return remote(part_buf.at[0, j], g_buf.at[2, j], g_send.at[1, j], g_recv.at[1, j], right)
-        return remote(part_buf.at[1, j], r_buf.at[2, j], r_send.at[1, j], r_recv.at[1, j], left)
+    def part_copy(which, core, j):
+        chip = (z + 1 if which == 0 else z + chips - 1) % chips
+        return remote(part_buf.at[which, j, core * rows:(core + 1) * rows, :], end_buf.at[which, c, j],
+                      p_send.at[which, core, j], p_recv.at[which, c, j], chip * 2 + core)
 
     def finish(j):
-        for which, near, end in ((0, chips - 2, chips - 1), (1, 1, 0)):
+        for which, near in ((0, chips - 2), (1, 1)):
             @pl.when(z == near)
             def _():
                 part_buf[which, j] = inverse(part_acc[which, j])
-                part_copy(which, j).start()
-
-        for which, acc, out, end in ((0, conv_acc, conv_ref, chips - 1), (1, gg_acc, gg_ref, 0)):
+                part_copy(which, 0, j).start()
+                part_copy(which, 1, j).start()
+
+        for which, acc, out in ((0, conv_acc, conv_ref), (1, gg_acc, gg_ref)):
             y_buf[which, j] = inverse(acc[j])
-
-            @pl.when(z == end)
-            def _():
-                part_copy(which, j).wait_recv()
-                y_buf[which, j] += (g_buf if which == 0 else r_buf)[2, j]
-
             y_copy(which, j).start()
             out[:, columns(c, j)] = y_buf[which, j, my_rows, :]
 
@@ -351,7 +355,7 @@
         def step(j, carry):
             @pl.when((z + 1 + s < chips) & ((z >= 1) | (s == 0)))
             def _():
-                r_copy(s, j).wait_recv()
+                own_wait(1, j) if s == 0 else r_copy(s, j).wait_recv()
                 if s < last_step:
                     @pl.when(z >= 2)
                     def _():
@@ -368,7 +372,7 @@
 
             @pl.when((z - 1 - s >= 0) & ((z <= chips - 2) | (s == 0)))
             def _():
-                g_copy(s, j).wait_recv()
+                own_wait(0, j) if s == 0 else g_copy(s, j).wait_recv()
                 if s < last_step:
                     @pl.when(z <= chips - 3)
                     def _():
@@ -396,8 +400,8 @@
     below = jnp.concatenate([turned[nf:, :block], jnp.zeros((nf, block), jnp.float32)], axis=0)
     sums = (turned[:, block:] + below) * (1.0 / block)
 
-    def c_copy(n):
-        return remote(c_own.at[n], c_buf.at[z], c_send.at[n], c_recv.at[z], n * 2 + c)
+    def c_copy(n, core):
+        return remote(c_own.at[n, core], c_buf.at[z, c], c_send.at[n, core], c_recv.at[z, c], n * 2 + core)
 
     my_reach = jnp.where(z == chips - 2, chips - 1, jnp.where(z == chips - 1, 1, z))
 
@@ -410,33 +414,45 @@
 
         @pl.when((n <= my_reach) & (n != z))
         def _():
-            c_copy(n).start()
-
+            c_copy(n, 0).start()
+            c_copy(n, 1).start()
+
+    c_copy(z, 1 - c).start()
+
+    def place(j, carry):
+        for which, out, end in ((0, conv_ref, chips - 1), (1, gg_ref, 0)):
+            y_copy(which, j).wait_recv()
+            out[:, columns(1 - c, j)] = x_buf[which, j]
+
+            @pl.when(z == end)
+            def _():
+                for core in range(2):
+                    remote(part_buf.at[which, j, :rows, :], end_buf.at[which, core, j],
+                           p_send.at[which, 0, j], p_recv.at[which, core, j], partner).wait_recv()
+                    out[:, columns(core, j)] += end_buf[which, core, j]
+        return carry
+
+    lax.fori_loop(0, chunks, place, 0)
+
+    def c_wait(chip, core):
+        remote(c_own.at[0, 0], c_buf.at[chip, core], c_send.at[0, 0], c_recv.at[chip, core], partner).wait_recv()
+
+    c_wait(z, 1 - c)
+    gf_ref[pl.ds(pl.multiple_of(c * nf, nf), nf), :] = c_own[z, c]
+    gf_ref[pl.ds(pl.multiple_of((1 - c) * nf, nf), nf), :] = c_buf[z, 1 - c]
     for i in range(1, chips):
         @pl.when((z <= reach(i)) & (i != z))
         def _():
-            remote(c_own.at[0], c_buf.at[i], c_send.at[0], c_recv.at[i], partner).wait_recv()
-            c_own[z] += c_buf[i]
-
-    last = remote(c_own.at[z, 1 - c], f_buf, p_send, p_recv, partner)
-    last.start()
-    gf_ref[pl.ds(pl.multiple_of(c * nf, nf), nf), :] = c_own[z, c]
-
-    def place(j, carry):
-        for which, out in ((0, conv_ref), (1, gg_ref)):
-            y_copy(which, j).wait_recv()
-            out[:, columns(1 - c, j)] = x_buf[which, j]
-        return carry
-
-    lax.fori_loop(0, chunks, place, 0)
-    last.wait_recv()
-    gf_ref[pl.ds(pl.multiple_of((1 - c) * nf, nf), nf), :] = f_buf[...]
-
-    last.wait_send()
+            for core in range(2):
+                c_wait(i, core)
+                gf_ref[core * nf:(core + 1) * nf, :] += c_buf[i, core]
+
+    c_copy(z, 1 - c).wait_send()
     for n in range(chips):
         @pl.when((n <= my_reach) & (n != z))
         def _():
-            c_copy(n).wait_send()
+            c_copy(n, 0).wait_send()
+            c_copy(n, 1).wait_send()
     for d in range(1, groups):
         filter_copy(d).wait_send()
 
@@ -444,19 +460,26 @@
         for which in range(2):
             swap(which, j).wait_send()
             y_copy(which, j).wait_send()
-        for s in range(last_step + 1):
-            @pl.when((z - s >= 0) & (z + 1 < (chips if s == 0 else chips - 1)))
+        for which, sends in ((0, z + 1 < chips), (1, z >= 1)):
+            @pl.when(sends)
+            def _():
+                own_copy(which, 0, j).wait_send()
+                own_copy(which, 1, j).wait_send()
+
+        for s in range(1, last_step + 1):
+            @pl.when((z - s >= 0) & (z + 1 < chips - 1))
             def _():
                 g_copy(s, j).wait_send()
 
-            @pl.when((z + s < chips) & (z >= (1 if s == 0 else 2)))
+            @pl.when((z + s < chips) & (z >= 2))
             def _():
                 r_copy(s, j).wait_send()
 
         for which, near in ((0, chips - 2), (1, 1)):
             @pl.when(z == near)
             def _():
-                part_copy(which, j).wait_send()
+                part_copy(which, 0, j).wait_send()
+                part_copy(which, 1, j).wait_send()
         return carry
 
     lax.fori_loop(0, chunks, drain, 0)
@@ -482,13 +505,13 @@
         (2, chunks, rows, LANES),
         (chips, 2, nf, rows),
         (chips, 2, nf, rows),
-        (nf, rows),
+        (2, 2, chunks, rows, LANES),
     ]
     steps = max(chips - 1, 1)
     sems = [
         (2 * chips,), (2 * chips,), (2, chunks), (2, chunks), (steps, chunks), (steps, chunks),
-        (steps, chunks), (steps, chunks), (2, chunks), (2, chunks), (chips,), (chips,),
-        (11,),
+        (steps, chunks), (steps, chunks), (2, chunks), (2, chunks), (chips, 2), (chips, 2),
+        (11,), (2, 2, chunks), (2, 2, chunks), (2, 2, chunks), (2, 2, chunks),
     ]
     used = sum(4 * math.prod(shape) for shape in memory)
     held = [((rows, 2 * half), jnp.bfloat16)] * 4 + [((2 * nf, rows), f32)]
@@ -497,7 +520,6 @@
     specs = [pltpu.VMEM(shape, kind) for shape, kind in held]
     specs += [pltpu.VMEM(shape, f32) for shape in memory]
     specs += [pltpu.SemaphoreType.DMA(shape) for shape in sems]
-    specs += [pltpu.SemaphoreType.DMA, pltpu.SemaphoreType.DMA]
     return used, specs
 
 
@@ -526,7 +548,7 @@
     _, scratches = scratch(chips, rows, half, nf)
     vmem = pl.BlockSpec(memory_space=pltpu.VMEM)
     conv, grad_gated, corr = pl.pallas_call(
-        functools.partial(kernel, chips),
+        functools.partial(kernel, chips, scale),
         out_shape=(
             jax.ShapeDtypeStruct((rows, width), jnp.float32),
             jax.ShapeDtypeStruct((rows, width), jnp.float32),
@@ -539,7 +561,7 @@
             collective_id=0, has_side_effects=True, vmem_limit_bytes=VMEM_LIMIT),
         cost_estimate=pl.CostEstimate(flops=10**10, bytes_accessed=8 * 2**20, transcendentals=0),
         name="ring_conv",
-    )(query_gate, key_gate, value_in, grad_out, (filter_raw * scale).T, *fwd, *inv, spread, gather)
+    )(query_gate, key_gate, value_in, grad_out, filter_raw.T, *fwd, *inv, spread, gather)
     output = (query_gate.astype(jnp.float32) * conv).astype(jnp.bfloat16)
     grad_query = (grad_out.astype(jnp.float32) * conv).astype(jnp.bfloat16)
     grad_key = (grad_gated * value_in.astype(jnp.float32)).astype(jnp.bfloat16)

time: 50.9 us -> 45.9 us (0.902)
  Pallas kernels: 45.6 us -> 42.1 us
  other arithmetic: 4.35 us -> 2.98 us
    pallas_call x1, Pallas kernels: 45.6 us -> 42.1 us  [local_fast(): pl.pallas_call(functools.partial(kernel, chips, scale), out_shape=(jax.Sh...]
    transpose x1 -> x0, other arithmetic: 1.38 us -> none  [local_fast(): conv, grad_gated, corr = pl.pallas_call(functools.partial(kernel, chips),...]
where the time goes in v4:
time: 45.9 us; the launch traced here: 45.8 us
  Pallas kernels  42.1 us (92%)
  other arithmetic  2.98 us (6%)
  between operations  0.71 us (2%)
    pallas_call x1, Pallas kernels, local_fast(): pl.pallas_call(functools.partial(kernel, chips, scale), out_shape=(jax.Sh...  42.1 us
    convert_element_type x1, other arithmetic, local_fast(): (grad_gated * key_gate.astype(jnp.float32)).astype(jnp.bfloat16)  2.36 us

profile of v4, /device:TPU:0, one launch (start us, length us, event | category | flops | bytes accessed | tf_op | source)
XLA Modules:
  0.0 45.8 jit_solution(8205227454921267624)
XLA Ops:
  0.6 0.0 copy-start
  0.6 0.0 copy-start.1
  0.7 0.0 copy-start.2
  0.7 0.0 copy-start.3
  0.7 42.1 %ring_conv.1 = (f32[128,1024]{1,0:T(8,128)}, f32[128,1024]{1,0:T(8,128)}, f32[64,128]{1,0:T(8,128)}) custom-call(bf16[128,1024]{1,0:T(8,128)(2,1)} %q_hbm.1, bf16[128,1024]{1,0:T(8,128)(2,1)} %k_hbm.1, bf16[128,1024]{1,0:T(8,128)(2,1)} %v_hbm.1, bf16[128,1024]{1,0:T(8,128)(2,1)} %go_hbm.1, f32[64,128]{1,0:T(8,128)} %bitcast.3, ...), custom_call_target="tpu_custom_call" | custom-call | flops 10000000000 | bytes 8388608 | tf_op jit(solution)/shard_map/ring_conv/pallas_call | solution.py:550
  42.7 0.0 copy-done
  42.8 0.0 copy-done.1
  42.8 0.0 copy-done.2
  42.8 0.0 copy-done.3
  42.8 0.0 copy-start.4
  42.8 2.4 %multiply_convert_fusion = (bf16[128,1024]{1,0:T(8,128)(2,1)}, bf16[128,1024]{1,0:T(8,128)(2,1)}, bf16[128,1024]{1,0:T(8,128)(2,1)}, bf16[128,1024]{1,0:T(8,128)(2,1)}) fusion(f32[128,1024]{1,0:T(8,128)} %get-tuple-element.9, bf16[128,1024]{1,0:T(8,128)(2,1)S(1)} %copy-done.1, bf16[128,1024]{1,0:T(8,128)(2,1)S(1)} %copy-done.2, ...), kind=kLoop, calls=%fused_computation | loop fusion | flops 1572864 | bytes 3145728 | tf_op jit(solution)/shard_map/convert_element_type | solution.py:568
  45.1 0.0 copy-done.4
  45.2 0.6 %multiply_bitcast_fusion = f32[128,64]{0,1:T(8,128)} fusion(f32[64,128]{1,0:T(8,128)S(1)} %copy-done.4), kind=kLoop, calls=%fused_computation.4 | loop fusion | flops 8192 | bytes 65536 | tf_op jit(solution)/shard_map/mul | solution.py:569
Async XLA Ops:
  0.6 42.1 %copy-start = (bf16[128,1024]{1,0:T(8,128)(2,1)S(1)}, bf16[128,1024]{1,0:T(8,128)(2,1)}, u32[]{:S(2)}) copy-start(bf16[128,1024]{1,0:T(8,128)(2,1)} %q_hbm.1) | copy-start | bytes 786436
  0.6 42.1 %copy-start.1 = (bf16[128,1024]{1,0:T(8,128)(2,1)S(1)}, bf16[128,1024]{1,0:T(8,128)(2,1)}, u32[]{:S(2)}) copy-start(bf16[128,1024]{1,0:T(8,128)(2,1)} %k_hbm.1) | copy-start | bytes 786436
  0.7 42.1 %copy-start.2 = (bf16[128,1024]{1,0:T(8,128)(2,1)S(1)}, bf16[128,1024]{1,0:T(8,128)(2,1)}, u32[]{:S(2)}) copy-start(bf16[128,1024]{1,0:T(8,128)(2,1)} %v_hbm.1) | copy-start | bytes 786436
  0.7 42.1 %copy-start.3 = (bf16[128,1024]{1,0:T(8,128)(2,1)S(1)}, bf16[128,1024]{1,0:T(8,128)(2,1)}, u32[]{:S(2)}) copy-start(bf16[128,1024]{1,0:T(8,128)(2,1)} %go_hbm.1) | copy-start | bytes 786436
  42.8 2.4 %copy-start.4 = (f32[64,128]{1,0:T(8,128)S(1)}, f32[64,128]{1,0:T(8,128)}, u32[]{:S(2)}) copy-start(f32[64,128]{1,0:T(8,128)} %get-tuple-element.10) | copy-start | bytes 98308

commit v5 on v4

--- a/solution.py
+++ b/solution.py
@@ -232,8 +232,27 @@
         part = pl.ds(pl.multiple_of((target % 2) * nf, nf), nf)
         return remote(filt_ref.at[part, :], h_buf.at[z, c], f_send.at[d], f_recv.at[d], target)
 
+    def wanted(source, target):
+        return (target <= chips - 2) & ((target >= 1) | (source <= 1))
+
+    def sends_filter(d):
+        return wanted(z, ((me + d) % groups) // 2)
+
+    def gets_filter(d):
+        return wanted(((me + groups - d) % groups) // 2, z)
+
+    def filter_pass():
+        return remote(h_buf.at[0:2], h_buf.at[0:2], f_send.at[0], f_recv.at[0], right)
+
     for d in range(1, groups):
-        filter_copy(d).start()
+        @pl.when(sends_filter(d))
+        def _():
+            filter_copy(d).start()
+
+    @pl.when((z == 0) | (z == chips - 1))
+    def _():
+        h_buf[2:] = jnp.zeros((chips - 2, 2, nf, rows), jnp.float32)
+
     h_buf[z, c] = filt_ref[pl.ds(pl.multiple_of(c * nf, nf), nf), :]
 
     def own_copy(which, other, j):
@@ -275,7 +294,17 @@
     for load in loads[5:]:
         load.wait()
     for d in range(1, groups):
-        filter_copy(d).wait_recv()
+        @pl.when(gets_filter(d))
+        def _():
+            filter_copy(d).wait_recv()
+
+    @pl.when(z == chips - 2)
+    def _():
+        filter_pass().start()
+
+    @pl.when(z == chips - 1)
+    def _():
+        filter_pass().wait_recv()
 
     lags = chips * nf
     taps = halves(jnp.concatenate(
@@ -353,30 +382,39 @@
     last_step = chips - 3
     for s in range(last_step + 1):
         def step(j, carry):
-            @pl.when((z + 1 + s < chips) & ((z >= 1) | (s == 0)))
+            r_here = (z + 1 + s < chips) & ((z >= 1) | (s == 0))
+            g_here = (z - 1 - s >= 0) & ((z <= chips - 2) | (s == 0))
+
+            @pl.when(r_here)
             def _():
                 own_wait(1, j) if s == 0 else r_copy(s, j).wait_recv()
                 if s < last_step:
                     @pl.when(z >= 2)
                     def _():
                         r_copy(s + 1, j).start()
-                r = spectrum(r_buf[s + 1, j])
-                gg_acc[j] += conj_times(h_spec[s + 1, j], r)
-                if s == 0:
-                    r_next[j] = r
-
-                @pl.when(z == 1)
-                def _():
-                    term = conj_times(h_spec[s + 2, j], r)
-                    part_acc[1, j] = term if s == 0 else part_acc[1, j] + term
-
-            @pl.when((z - 1 - s >= 0) & ((z <= chips - 2) | (s == 0)))
+
+            @pl.when(g_here)
             def _():
                 own_wait(0, j) if s == 0 else g_copy(s, j).wait_recv()
                 if s < last_step:
                     @pl.when(z <= chips - 3)
                     def _():
                         g_copy(s + 1, j).start()
+
+            @pl.when(r_here)
+            def _():
+                r = spectrum(r_buf[s + 1, j])
+                gg_acc[j] += conj_times(h_spec[s + 1, j], r)
+                if s == 0:
+                    r_next[j] = r
+
+                @pl.when(z == 1)
+                def _():
+                    term = conj_times(h_spec[s + 2, j], r)
+                    part_acc[1, j] = term if s == 0 else part_acc[1, j] + term
+
+            @pl.when(g_here)
+            def _():
                 g = spectrum(g_buf[s + 1, j])
                 conv_acc[j] += times(h_spec[s + 1, j], g)
                 add_corr(s + 1, j, g, r_spec[j])
@@ -454,7 +492,13 @@
             c_copy(n, 0).wait_send()
             c_copy(n, 1).wait_send()
     for d in range(1, groups):
-        filter_copy(d).wait_send()
+        @pl.when(sends_filter(d))
+        def _():
+            filter_copy(d).wait_send()
+
+    @pl.when(z == chips - 2)
+    def _():
+        filter_pass().wait_send()
 
     def drain(j, carry):
         for which in range(2):

time: 45.9 us -> 43.9 us (0.956)
  Pallas kernels: 42.1 us -> 40 us
    pallas_call x1, Pallas kernels: 42.1 us -> 40 us  [local_fast(): pl.pallas_call(functools.partial(kernel, chips, scale), out_shape=(jax.Sh...]
where the time goes in v5:
time: 43.9 us; the launch traced here: 43.7 us
  Pallas kernels  40 us (91%)
  other arithmetic  2.98 us (7%)
  between operations  0.71 us (2%)
    pallas_call x1, Pallas kernels, local_fast(): pl.pallas_call(functools.partial(kernel, chips, scale), out_shape=(jax.Sh...  40 us
    convert_element_type x1, other arithmetic, local_fast(): (grad_gated * key_gate.astype(jnp.float32)).astype(jnp.bfloat16)  2.36 us

profile of v5, /device:TPU:0, one launch (start us, length us, event | category | flops | bytes accessed | tf_op | source)
XLA Modules:
  0.0 43.7 jit_solution(5684431405202188912)
XLA Ops:
  0.6 0.0 copy-start
  0.6 0.0 copy-start.1
  0.7 0.0 copy-start.2
  0.7 0.0 copy-start.3
  0.7 40.0 %ring_conv.1 = (f32[128,1024]{1,0:T(8,128)}, f32[128,1024]{1,0:T(8,128)}, f32[64,128]{1,0:T(8,128)}) custom-call(bf16[128,1024]{1,0:T(8,128)(2,1)} %q_hbm.1, bf16[128,1024]{1,0:T(8,128)(2,1)} %k_hbm.1, bf16[128,1024]{1,0:T(8,128)(2,1)} %v_hbm.1, bf16[128,1024]{1,0:T(8,128)(2,1)} %go_hbm.1, f32[64,128]{1,0:T(8,128)} %bitcast.3, ...), custom_call_target="tpu_custom_call" | custom-call | flops 10000000000 | bytes 8388608 | tf_op jit(solution)/shard_map/ring_conv/pallas_call | solution.py:594
  40.7 0.0 copy-done
  40.7 0.0 copy-done.1
  40.7 0.0 copy-done.2
  40.7 0.0 copy-done.3
  40.7 0.0 copy-start.4
  40.8 2.4 %multiply_convert_fusion = (bf16[128,1024]{1,0:T(8,128)(2,1)}, bf16[128,1024]{1,0:T(8,128)(2,1)}, bf16[128,1024]{1,0:T(8,128)(2,1)}, bf16[128,1024]{1,0:T(8,128)(2,1)}) fusion(f32[128,1024]{1,0:T(8,128)} %get-tuple-element.9, bf16[128,1024]{1,0:T(8,128)(2,1)S(1)} %copy-done.1, bf16[128,1024]{1,0:T(8,128)(2,1)S(1)} %copy-done.2, ...), kind=kLoop, calls=%fused_computation | loop fusion | flops 1572864 | bytes 3145728 | tf_op jit(solution)/shard_map/convert_element_type | solution.py:612
  43.1 0.0 copy-done.4
  43.1 0.6 %multiply_bitcast_fusion = f32[128,64]{0,1:T(8,128)} fusion(f32[64,128]{1,0:T(8,128)S(1)} %copy-done.4), kind=kLoop, calls=%fused_computation.4 | loop fusion | flops 8192 | bytes 65536 | tf_op jit(solution)/shard_map/mul | solution.py:613
Async XLA Ops:
  0.6 40.1 %copy-start = (bf16[128,1024]{1,0:T(8,128)(2,1)S(1)}, bf16[128,1024]{1,0:T(8,128)(2,1)}, u32[]{:S(2)}) copy-start(bf16[128,1024]{1,0:T(8,128)(2,1)} %q_hbm.1) | copy-start | bytes 786436
  0.6 40.1 %copy-start.1 = (bf16[128,1024]{1,0:T(8,128)(2,1)S(1)}, bf16[128,1024]{1,0:T(8,128)(2,1)}, u32[]{:S(2)}) copy-start(bf16[128,1024]{1,0:T(8,128)(2,1)} %k_hbm.1) | copy-start | bytes 786436
  0.7 40.1 %copy-start.2 = (bf16[128,1024]{1,0:T(8,128)(2,1)S(1)}, bf16[128,1024]{1,0:T(8,128)(2,1)}, u32[]{:S(2)}) copy-start(bf16[128,1024]{1,0:T(8,128)(2,1)} %v_hbm.1) | copy-start | bytes 786436
  0.7 40.1 %copy-start.3 = (bf16[128,1024]{1,0:T(8,128)(2,1)S(1)}, bf16[128,1024]{1,0:T(8,128)(2,1)}, u32[]{:S(2)}) copy-start(bf16[128,1024]{1,0:T(8,128)(2,1)} %go_hbm.1) | copy-start | bytes 786436
  40.7 2.4 %copy-start.4 = (f32[64,128]{1,0:T(8,128)S(1)}, f32[64,128]{1,0:T(8,128)}, u32[]{:S(2)}) copy-start(f32[64,128]{1,0:T(8,128)} %get-tuple-element.10) | copy-start | bytes 98308

commit v6 on v5

--- a/solution.py
+++ b/solution.py
@@ -366,20 +366,23 @@
         return remote(part_buf.at[which, j, core * rows:(core + 1) * rows, :], end_buf.at[which, c, j],
                       p_send.at[which, core, j], p_recv.at[which, c, j], chip * 2 + core)
 
+    def add_part(which, s, j, term):
+        total = term if s == 0 else part_acc[which, j] + term
+        if s < last_step:
+            part_acc[which, j] = total
+        else:
+            part_buf[which, j] = inverse(total)
+            part_copy(which, 0, j).start()
+            part_copy(which, 1, j).start()
+
+    last_step = chips - 3
+
     def finish(j):
-        for which, near in ((0, chips - 2), (1, 1)):
-            @pl.when(z == near)
-            def _():
-                part_buf[which, j] = inverse(part_acc[which, j])
-                part_copy(which, 0, j).start()
-                part_copy(which, 1, j).start()
-
         for which, acc, out in ((0, conv_acc, conv_ref), (1, gg_acc, gg_ref)):
             y_buf[which, j] = inverse(acc[j])
             y_copy(which, j).start()
             out[:, columns(c, j)] = y_buf[which, j, my_rows, :]
 
-    last_step = chips - 3
     for s in range(last_step + 1):
         def step(j, carry):
             r_here = (z + 1 + s < chips) & ((z >= 1) | (s == 0))
@@ -404,25 +407,28 @@
             @pl.when(r_here)
             def _():
                 r = spectrum(r_buf[s + 1, j])
+
+                @pl.when(z == 1)
+                def _():
+                    add_part(1, s, j, conj_times(h_spec[s + 2, j], r))
+
                 gg_acc[j] += conj_times(h_spec[s + 1, j], r)
                 if s == 0:
                     r_next[j] = r
 
-                @pl.when(z == 1)
+            @pl.when(g_here)
+            def _():
+                g = spectrum(g_buf[s + 1, j])
+
+                @pl.when(z == chips - 2)
                 def _():
-                    term = conj_times(h_spec[s + 2, j], r)
-                    part_acc[1, j] = term if s == 0 else part_acc[1, j] + term
-
-            @pl.when(g_here)
-            def _():
-                g = spectrum(g_buf[s + 1, j])
+                    add_part(0, s, j, times(h_spec[s + 2, j], g))
+
                 conv_acc[j] += times(h_spec[s + 1, j], g)
                 add_corr(s + 1, j, g, r_spec[j])
 
                 @pl.when(z == chips - 2)
                 def _():
-                    term = times(h_spec[s + 2, j], g)
-                    part_acc[0, j] = term if s == 0 else part_acc[0, j] + term
                     add_corr(s + 2, j, g, r_next[j])
 
             if s == last_step:

time: 43.9 us -> 43.8 us (level)
  no operation moved by 1% of the time
where the time goes in v6:
time: 43.8 us; the launch traced here: 43.7 us
  Pallas kernels  40 us (91%)
  other arithmetic  2.98 us (7%)
  between operations  0.71 us (2%)
    pallas_call x1, Pallas kernels, local_fast(): pl.pallas_call(functools.partial(kernel, chips, scale), out_shape=(jax.Sh...  40 us
    convert_element_type x1, other arithmetic, local_fast(): (grad_gated * key_gate.astype(jnp.float32)).astype(jnp.bfloat16)  2.36 us

profile of v6, /device:TPU:0, one launch (start us, length us, event | category | flops | bytes accessed | tf_op | source)
XLA Modules:
  0.0 43.7 jit_solution(10826558639850900006)
XLA Ops:
  0.6 0.0 copy-start
  0.6 0.0 copy-start.1
  0.7 0.0 copy-start.2
  0.7 0.0 copy-start.3
  0.7 40.0 %ring_conv.1 = (f32[128,1024]{1,0:T(8,128)}, f32[128,1024]{1,0:T(8,128)}, f32[64,128]{1,0:T(8,128)}) custom-call(bf16[128,1024]{1,0:T(8,128)(2,1)} %q_hbm.1, bf16[128,1024]{1,0:T(8,128)(2,1)} %k_hbm.1, bf16[128,1024]{1,0:T(8,128)(2,1)} %v_hbm.1, bf16[128,1024]{1,0:T(8,128)(2,1)} %go_hbm.1, f32[64,128]{1,0:T(8,128)} %bitcast.3, ...), custom_call_target="tpu_custom_call" | custom-call | flops 10000000000 | bytes 8388608 | tf_op jit(solution)/shard_map/ring_conv/pallas_call | solution.py:600
  40.7 0.0 copy-done
  40.7 0.0 copy-done.1
  40.7 0.0 copy-done.2
  40.7 0.0 copy-done.3
  40.7 0.0 copy-start.4
  40.7 2.4 %multiply_convert_fusion = (bf16[128,1024]{1,0:T(8,128)(2,1)}, bf16[128,1024]{1,0:T(8,128)(2,1)}, bf16[128,1024]{1,0:T(8,128)(2,1)}, bf16[128,1024]{1,0:T(8,128)(2,1)}) fusion(f32[128,1024]{1,0:T(8,128)} %get-tuple-element.9, bf16[128,1024]{1,0:T(8,128)(2,1)S(1)} %copy-done.1, bf16[128,1024]{1,0:T(8,128)(2,1)S(1)} %copy-done.2, ...), kind=kLoop, calls=%fused_computation | loop fusion | flops 1572864 | bytes 3145728 | tf_op jit(solution)/shard_map/convert_element_type | solution.py:618
  43.1 0.0 copy-done.4
  43.1 0.6 %multiply_bitcast_fusion = f32[128,64]{0,1:T(8,128)} fusion(f32[64,128]{1,0:T(8,128)S(1)} %copy-done.4), kind=kLoop, calls=%fused_computation.4 | loop fusion | flops 8192 | bytes 65536 | tf_op jit(solution)/shard_map/mul | solution.py:619
Async XLA Ops:
  0.6 40.0 %copy-start = (bf16[128,1024]{1,0:T(8,128)(2,1)S(1)}, bf16[128,1024]{1,0:T(8,128)(2,1)}, u32[]{:S(2)}) copy-start(bf16[128,1024]{1,0:T(8,128)(2,1)} %q_hbm.1) | copy-start | bytes 786436
  0.6 40.0 %copy-start.1 = (bf16[128,1024]{1,0:T(8,128)(2,1)S(1)}, bf16[128,1024]{1,0:T(8,128)(2,1)}, u32[]{:S(2)}) copy-start(bf16[128,1024]{1,0:T(8,128)(2,1)} %k_hbm.1) | copy-start | bytes 786436
  0.7 40.0 %copy-start.2 = (bf16[128,1024]{1,0:T(8,128)(2,1)S(1)}, bf16[128,1024]{1,0:T(8,128)(2,1)}, u32[]{:S(2)}) copy-start(bf16[128,1024]{1,0:T(8,128)(2,1)} %v_hbm.1) | copy-start | bytes 786436
  0.7 40.0 %copy-start.3 = (bf16[128,1024]{1,0:T(8,128)(2,1)S(1)}, bf16[128,1024]{1,0:T(8,128)(2,1)}, u32[]{:S(2)}) copy-start(bf16[128,1024]{1,0:T(8,128)(2,1)} %go_hbm.1) | copy-start | bytes 786436
  40.7 2.4 %copy-start.4 = (f32[64,128]{1,0:T(8,128)S(1)}, f32[64,128]{1,0:T(8,128)}, u32[]{:S(2)}) copy-start(f32[64,128]{1,0:T(8,128)} %get-tuple-element.10) | copy-start | bytes 98308

commit v7 on v6

--- a/solution.py
+++ b/solution.py
@@ -169,7 +169,7 @@
 
 
 def kernel(chips, scale, q_hbm, k_hbm, v_hbm, go_hbm, filt_hbm, fwd_hi_hbm, fwd_lo_hbm, inv_hi_hbm, inv_lo_hbm, spread_hbm, gather_hbm,
-           conv_ref, gg_ref, gf_ref,
+           out_ref, gq_ref, gk_ref, gv_ref, gf_ref, conv_ref, gg_ref,
            q_ref, k_ref, v_ref, go_ref, filt_ref, fwd_hi, fwd_lo, inv_hi, inv_lo, spread_ref, gather_ref,
            g_buf, r_buf, sg_buf, h_buf, h_spec, conv_acc, gg_acc, r_spec, r_next, part_acc, part_buf, c_spec, y_buf, x_buf, c_own, c_buf, end_buf,
            f_send, f_recv, e_send, e_recv, g_send, g_recv, r_send, r_recv, y_send, y_recv, c_send, c_recv, load_sem, o_send, o_recv, p_send, p_recv):
@@ -474,6 +474,14 @@
                     remote(part_buf.at[which, j, :rows, :], end_buf.at[which, core, j],
                            p_send.at[which, 0, j], p_recv.at[which, core, j], partner).wait_recv()
                     out[:, columns(core, j)] += end_buf[which, core, j]
+
+        for core in range(2):
+            cols = columns(core, j)
+            conv, grad = conv_ref[:, cols], gg_ref[:, cols]
+            out_ref[:, cols] = (q_ref[:, cols].astype(jnp.float32) * conv).astype(jnp.bfloat16)
+            gq_ref[:, cols] = (go_ref[:, cols].astype(jnp.float32) * conv).astype(jnp.bfloat16)
+            gk_ref[:, cols] = (grad * v_ref[:, cols].astype(jnp.float32)).astype(jnp.bfloat16)
+            gv_ref[:, cols] = (grad * k_ref[:, cols].astype(jnp.float32)).astype(jnp.bfloat16)
         return carry
 
     lax.fori_loop(0, chunks, place, 0)
@@ -564,7 +572,7 @@
         (11,), (2, 2, chunks), (2, 2, chunks), (2, 2, chunks), (2, 2, chunks),
     ]
     used = sum(4 * math.prod(shape) for shape in memory)
-    held = [((rows, 2 * half), jnp.bfloat16)] * 4 + [((2 * nf, rows), f32)]
+    held = [((rows, 2 * half), f32)] * 2 + [((rows, 2 * half), jnp.bfloat16)] * 4 + [((2 * nf, rows), f32)]
     held += [((2 * block, 2 * block), jnp.bfloat16)] * 2 + [((block, 2 * block), jnp.bfloat16)] * 2
     held += [((chips, 2 * chips * nf, half), jnp.bfloat16), ((chips, chunks, 2 * LANES, chips * nf), jnp.bfloat16)]
     specs = [pltpu.VMEM(shape, kind) for shape, kind in held]
@@ -597,26 +605,21 @@
     gather = np.tile(gather, (1, 1, 2, 1)).astype(jnp.bfloat16)
     _, scratches = scratch(chips, rows, half, nf)
     vmem = pl.BlockSpec(memory_space=pltpu.VMEM)
-    conv, grad_gated, corr = pl.pallas_call(
+    *gates, corr = pl.pallas_call(
         functools.partial(kernel, chips, scale),
         out_shape=(
-            jax.ShapeDtypeStruct((rows, width), jnp.float32),
-            jax.ShapeDtypeStruct((rows, width), jnp.float32),
+            *[jax.ShapeDtypeStruct((rows, width), jnp.bfloat16)] * 4,
             jax.ShapeDtypeStruct((filters, rows), jnp.float32),
         ),
         in_specs=[pl.BlockSpec(memory_space=pltpu.HBM)] * 11,
-        out_specs=(vmem,) * 3,
+        out_specs=(vmem,) * 5,
         scratch_shapes=scratches,
         compiler_params=pltpu.CompilerParams(
             collective_id=0, has_side_effects=True, vmem_limit_bytes=VMEM_LIMIT),
         cost_estimate=pl.CostEstimate(flops=10**10, bytes_accessed=8 * 2**20, transcendentals=0),
         name="ring_conv",
     )(query_gate, key_gate, value_in, grad_out, filter_raw.T, *fwd, *inv, spread, gather)
-    output = (query_gate.astype(jnp.float32) * conv).astype(jnp.bfloat16)
-    grad_query = (grad_out.astype(jnp.float32) * conv).astype(jnp.bfloat16)
-    grad_key = (grad_gated * value_in.astype(jnp.float32)).astype(jnp.bfloat16)
-    grad_value = (grad_gated * key_gate.astype(jnp.float32)).astype(jnp.bfloat16)
-    return output, grad_query, grad_key, grad_value, corr.T * scale
+    return *gates, corr.T * scale
 
 
 def dispatch(query_gate, key_gate, value_in, filter_raw, grad_out):

time: 43.8 us -> 46.7 us (1.066)
  local copies, waits for them, and re-layouts: 0.02 us -> 4.5 us
  other arithmetic: 2.98 us -> 1.38 us
    unnamed x10, local copies, waits for them, and re-layouts: 0.02 us -> 4.5 us
    convert_element_type x1 -> x0, other arithmetic: 2.36 us -> none  [local_fast(): (grad_gated * key_gate.astype(jnp.float32)).astype(jnp.bfloat16)]
    mul x1, other arithmetic: 0.62 us -> 1.38 us  [local_fast(): return (*gates, corr.T * scale)]
where the time goes in v7:
time: 46.7 us; the launch traced here: 46.5 us
  Pallas kernels  39.9 us (85%)
  local copies, waits for them, and re-layouts  4.5 us (10%)
  other arithmetic  1.38 us (3%)
  between operations  0.65 us (1%)
    pallas_call x1, Pallas kernels, local_fast(): pl.pallas_call(functools.partial(kernel, chips, scale), out_shape=(*[jax....  39.9 us
    unnamed x10, local copies, waits for them, and re-layouts  4.5 us
    mul x1, other arithmetic, local_fast(): return (*gates, corr.T * scale)  1.38 us

profile of v7, /device:TPU:0, one launch (start us, length us, event | category | flops | bytes accessed | tf_op | source)
XLA Modules:
  0.0 46.5 jit_solution(5349121239330017808)
XLA Ops:
  0.6 39.9 %ring_conv.1 = (bf16[128,1024]{1,0:T(8,128)(2,1)}, bf16[128,1024]{1,0:T(8,128)(2,1)}, bf16[128,1024]{1,0:T(8,128)(2,1)}, bf16[128,1024]{1,0:T(8,128)(2,1)}, f32[64,128]{1,0:T(8,128)}) custom-call(bf16[128,1024]{1,0:T(8,128)(2,1)} %q_hbm.1, bf16[128,1024]{1,0:T(8,128)(2,1)} %k_hbm.1, bf16[128,1024]{1,0:T(8,128)(2,1)} %v_hbm.1, bf16[128,1024]{1,0:T(8,128)(2,1)} %go_hbm.1, ...), custom_call_target="tpu_custom_call" | custom-call | flops 10000000000 | bytes 8388608 | tf_op jit(solution)/shard_map/ring_conv/pallas_call | solution.py:608
  40.6 1.4 %multiply_bitcast_fusion = f32[128,64]{0,1:T(8,128)} fusion(f32[64,128]{1,0:T(8,128)} %get-tuple-element.14), kind=kLoop, calls=%fused_computation | loop fusion | flops 8192 | bytes 65536 | tf_op jit(solution)/shard_map/mul | solution.py:622
  42.0 0.0 copy-start.2
  42.0 1.7 %copy.20 = bf16[128,1024]{1,0:T(8,128)(2,1)} copy(bf16[128,1024]{1,0:T(8,128)(2,1)} %get-tuple-element.20) | data formatting | bytes 524288
  43.7 0.0 copy-done.2
  43.7 0.0 copy-start.1
  43.7 0.7 %copy.21 = bf16[128,1024]{1,0:T(8,128)(2,1)} copy(bf16[128,1024]{1,0:T(8,128)(2,1)S(1)} %copy-done.2) | data formatting | bytes 524288
  44.4 0.3 copy-done.1
  44.7 0.0 copy-start
  44.7 0.7 %copy.22 = bf16[128,1024]{1,0:T(8,128)(2,1)} copy(bf16[128,1024]{1,0:T(8,128)(2,1)S(1)} %copy-done.1) | data formatting | bytes 524288
  45.4 0.3 copy-done
  45.8 0.7 %copy.23 = bf16[128,1024]{1,0:T(8,128)(2,1)} copy(bf16[128,1024]{1,0:T(8,128)(2,1)S(1)} %copy-done) | data formatting | bytes 524288
Async XLA Ops:
  42.0 1.7 %copy-start.2 = (bf16[128,1024]{1,0:T(8,128)(2,1)S(1)}, bf16[128,1024]{1,0:T(8,128)(2,1)}, u32[]{:S(2)}) copy-start(bf16[128,1024]{1,0:T(8,128)(2,1)} %get-tuple-element.21) | copy-start | bytes 786436
  43.7 1.0 %copy-start.1 = (bf16[128,1024]{1,0:T(8,128)(2,1)S(1)}, bf16[128,1024]{1,0:T(8,128)(2,1)}, u32[]{:S(2)}) copy-start(bf16[128,1024]{1,0:T(8,128)(2,1)} %get-tuple-element.22) | copy-start | bytes 786436
  44.7 1.0 %copy-start = (bf16[128,1024]{1,0:T(8,128)(2,1)S(1)}, bf16[128,1024]{1,0:T(8,128)(2,1)}, u32[]{:S(2)}) copy-start(bf16[128,1024]{1,0:T(8,128)(2,1)} %get-tuple-element.23) | copy-start | bytes 786436
